TPU v7x, 32 devices: a whole 2x2x4 slice. The times are simulated.
32 devices in a mesh: wave: 4 (over z), lat: 8 (over y, x, core).
Axes of the slice: x: 2, y: 2, z: 4, core: 2. Of those that a mesh axis runs over, the one named last changes fastest.
Arguments:
- spectral: bfloat16 [2, 16, 131328], P(None, None, 'wave'), may hold values from -6 to 6
- legendre: bfloat16 [32, 131328], P('lat', 'wave'), may hold values from -0.375 to 0.375
- wave_of_slot: int32 [512], replicated, may hold values from 3488 to 3999, as said below
- row_points: int32 [8, 4], P('lat'), may hold values from 20 to 16016, as said below
- quad_weight: float32 [8, 4], P('lat'), may hold values from 0.2 to 1
- grid_factor: float32 [8, 4, 16016], P('lat'), may hold values from 0.5 to 2
Outputs:
- spectral_out: float32 [2, 16, 131328], P(None, None, 'wave')
Inputs may be any that keep to these rules, and one draw needn't show every extreme that they name: `wave_of_slot`: slots 2 q and 2 q + 1 hold the wavenumbers 3488 + k and 3999 - k for one k of 0 to 255, each k once, so every owner holds 64 such pairs. `row_points`: each row has 20 + 4 min(i, 7999 - i) points for a latitude index i of the grid, the indices distinct over the rows; some row has 16016 points.
All inputs are finite; a program needn't handle non-finite values.
Results may differ from a plain program's by a relative error of at most 0.0024.
Values may be sent and summed in bfloat16 or wider, within the bound.
A program may use at most 64 MiB of HBM per device.

v0:
```python
import math

import jax
import jax.numpy as jnp
from jax import lax
from jax.sharding import PartitionSpec as P

TRUNC = 3999
M0 = 3488
MS = 512


block_width = 1024


def phase_tables(count, start, length, limit, first, inner, outer):
    k = start + jnp.arange(length, dtype=jnp.int32)
    valid = k < limit

    def table(mult):
        turns = mult[:, None] * k[None, :] % count
        angle = turns.astype(jnp.float32) * (2.0 * math.pi) / count.astype(jnp.float32)
        return (
            jnp.where(valid[None, :], jnp.cos(angle), 0.0),
            jnp.where(valid[None, :], jnp.sin(angle), 0.0),
        )

    inner_cos, inner_sin = table(jnp.arange(inner, dtype=jnp.int32))
    outer_cos, outer_sin = table(first + inner * jnp.arange(outer, dtype=jnp.int32))
    return (inner_cos, inner_sin, outer_cos, outer_sin)


def synthesize(real_part, imag_part, tables):
    inner_cos, inner_sin, outer_cos, outer_sin = tables
    outer = outer_cos.shape[0]
    inner = inner_cos.shape[0]
    width = inner_cos.shape[1]
    levels = real_part.shape[1]
    stacked = jnp.concatenate(
        [real_part.reshape(outer, inner, levels), imag_part.reshape(outer, inner, levels)], axis=1
    )
    left = stacked.transpose(0, 2, 1).reshape(outer * levels, 2 * inner)
    right = jnp.concatenate(
        [jnp.concatenate([inner_cos, inner_sin], 1), jnp.concatenate([-inner_sin, inner_cos], 1)], 0
    )
    mixed = jnp.dot(left, right, precision=lax.Precision.HIGH, preferred_element_type=jnp.float32)
    part_re = mixed[:, :width].reshape(outer, levels, width)
    part_im = mixed[:, width:].reshape(outer, levels, width)
    return jnp.sum(part_re * outer_cos[:, None, :] - part_im * outer_sin[:, None, :], axis=0)


def analyse(field, tables):
    inner_cos, inner_sin, outer_cos, outer_sin = tables
    outer = outer_cos.shape[0]
    inner = inner_cos.shape[0]
    width = inner_cos.shape[1]
    levels = field.shape[0]
    rotated_re = field[None, :, :] * outer_cos[:, None, :]
    rotated_im = -field[None, :, :] * outer_sin[:, None, :]
    left = jnp.concatenate([rotated_re, rotated_im], axis=2).reshape(outer * levels, 2 * width)
    right = jnp.concatenate(
        [
            jnp.concatenate([inner_cos.T, -inner_sin.T], 1),
            jnp.concatenate([inner_sin.T, inner_cos.T], 1),
        ],
        0,
    )
    mixed = jnp.dot(left, right, precision=lax.Precision.HIGH, preferred_element_type=jnp.float32)
    coef_re = (
        mixed[:, :inner]
        .reshape(outer, levels, inner)
        .transpose(0, 2, 1)
        .reshape(outer * inner, levels)
    )
    coef_im = (
        mixed[:, inner:]
        .reshape(outer, levels, inner)
        .transpose(0, 2, 1)
        .reshape(outer * inner, levels)
    )
    return (coef_re, coef_im)


def transform(by_wave, count, upper, factor_row):
    levels = by_wave.shape[1] // 2
    padded_row = jnp.pad(factor_row, (0, block_width))
    blocks = (upper + block_width - 1) // block_width

    def step(index, totals):
        start = index * block_width
        tables = phase_tables(count, start, block_width, upper, M0, 32, MS // 32)
        field = synthesize(by_wave[:, :levels], by_wave[:, levels:], tables)
        factor_part = lax.dynamic_slice_in_dim(padded_row, start, block_width)
        coef_re, coef_im = analyse(field * factor_part[None, :], tables)
        return (totals[0] + coef_re, totals[1] + coef_im)

    zeros_part = jnp.zeros((MS, levels), jnp.float32)
    totals = lax.fori_loop(0, blocks, step, (zeros_part, zeros_part))
    return jnp.concatenate([totals[0], totals[1]], 1)


def on_device(spectral, legendre, wave_of_slot, row_points, quad_weight, grid_factor):
    levels = spectral.shape[1]
    chans = 2 * levels
    owners = lax.axis_size("wave")
    per_owner = wave_of_slot.shape[0] // owners
    pairs = per_owner // 2
    group = legendre.shape[0]
    own = legendre.shape[1]
    span = own // pairs
    me = lax.axis_index("wave")
    mine = lax.dynamic_slice_in_dim(wave_of_slot, me * per_owner, per_owner)
    first_len = TRUNC + 1 - mine.reshape(pairs, 2)[:, 0]
    low_mask = jnp.arange(span, dtype=jnp.int32)[None, :] < first_len[:, None]
    coeffs = spectral.reshape(chans, pairs, span)
    blank = jnp.zeros_like(coeffs)
    low_coef = jnp.where(low_mask[None], coeffs, blank)
    high_coef = jnp.where(low_mask[None], blank, coeffs)
    row_leg = legendre.reshape(group, pairs, span)
    four_low = jnp.einsum("rqj,cqj->rqc", row_leg, low_coef, preferred_element_type=jnp.float32)
    four_high = jnp.einsum("rqj,cqj->rqc", row_leg, high_coef, preferred_element_type=jnp.float32)
    fourier = (
        jnp.stack([four_low, four_high], 2).reshape(group, per_owner, chans).astype(jnp.bfloat16)
    )
    position = wave_of_slot - M0
    points = row_points[0]
    weights = quad_weight[0]
    factors = grid_factor[0]
    ladder = jnp.arange(owners, dtype=jnp.int32)
    arrived = lax.all_to_all(fourier, "wave", split_axis=0, concat_axis=1, tiled=True)
    by_wave = jnp.zeros((MS, chans), jnp.float32).at[position].set(arrived[0].astype(jnp.float32))
    count = points[me]
    factor_row = lax.dynamic_index_in_dim(factors, me, 0, keepdims=False)
    kept = transform(by_wave, count, count, factor_row)
    scale = weights[me] / points[me].astype(jnp.float32)
    back = (kept * scale).astype(jnp.bfloat16)[position]
    returned = lax.all_to_all(back[None], "wave", split_axis=1, concat_axis=0, tiled=True)
    returned = jnp.take(returned, ladder, axis=0)
    split_back = returned.reshape(group, pairs, 2, chans)
    part_low = jnp.einsum(
        "rqj,rqc->cqj", row_leg, split_back[:, :, 0], preferred_element_type=jnp.float32
    )
    part_high = jnp.einsum(
        "rqj,rqc->cqj", row_leg, split_back[:, :, 1], preferred_element_type=jnp.float32
    )
    partial_value = jnp.where(low_mask[None], part_low, part_high).reshape(chans, own)
    total = lax.psum(partial_value, "lat")
    return total.reshape(2, levels, own)


def solution(mesh):
    return jax.shard_map(
        on_device,
        mesh=mesh,
        in_specs=(
            P(None, None, "wave"),
            P("lat", "wave"),
            P(),
            P("lat", None),
            P("lat", None),
            P("lat", None, None),
        ),
        out_specs=P(None, None, "wave"),
        check_vma=False,
    )
```

profile of v0, /device:TPU:0, one launch (start us, length us, event | category | flops | bytes accessed | tf_op | source)
XLA Modules:
  0.0 381.2 jit_solution(7728060948548864648)
XLA Ops:
  7.7 1.6 reshape.258
  9.3 5.8 %reshape.257 = bf16[32,64,513]{2,1,0:T(8,128)(2,1)S(1)} reshape(bf16[2,16,32832]{2,1,0:T(8,128)(2,1)} %param.8) | data formatting | bytes 4202496 | tf_op jit(solution)/shard_map/reshape | solution.py:115
  15.1 1.9 fusion.59
  17.0 1.9 fusion.62
  19.9 6.3 %all-to-all-start = ((bf16[4,128,32]{1,2,0:T(8,128)(2,1)}), bf16[4,128,32]{1,2,0:T(8,128)(2,1)S(1)}, u32[]{:S(2)}, u32[]{:S(2)}) async-start(bf16[4,128,32]{1,2,0:T(8,128)(2,1)} %copy.125), calls=%async_computation | async-start | bytes 65536 | tf_op jit(solution)/shard_map/all_to_all | solution.py:130
  30.7 1.1 all-to-all-done
  32.0 1.8 scatter_custom_fusion
  34.3 43.5 %while.14 = (s32[]{:T(128)}, f32[512,16]{0,1:T(8,128)S(1)}, f32[512,16]{0,1:T(8,128)S(1)}, s32[]{:T(128)}, s32[]{:T(128)}, /*index=5*/s32[]{:T(128)}, pred[]{:T(...) while((s32[]{:T(128)}, f32[512,16]{0,1:T(8,128)S(1)}, ...), condition=%wide.region_3.4_spmd, body=%wide.region_1.3_spmd.sunk | while | flops 406703136 | bytes 15827294 | solution.py:98
  35.2 1.0 cosine_select_fusion.4
  36.2 1.8 sine_select_fusion.4
  38.0 7.1 %fusion.96 = (f32[1024,32]{1,0:T(8,128)S(1)}, f32[1024,32]{1,0:T(8,128)S(1)}, f32[1024,32]{1,0:T(8,128)S(1)}) fusion(f32[]{:T(128)} %get-tuple-element.338, pred[]{:T(512)} %get-tuple-element.337, s32[]{:T(128)} %get-tuple-element.336, s32[1024]{0:T(1024)S(1)} %iota_add_fusion.2, pred[1024]{0:T(1024)(128)(4,1)S(1)} %broadcast_compare_fusion.2), kind=kLoop, calls=%fused_computation.37.clone.1 | loop fusion | flops 458752 | bytes 398345 | tf_op jit(solution)/shard_map/while/body/neg | solution.py:63
  45.1 1.0 convolution_bitcast_fusion.2
  46.8 1.5 fusion.97
  49.6 1.0 cosine_select_fusion.4
  50.5 1.8 sine_select_fusion.4
  52.3 7.1 %fusion.96 = (f32[1024,32]{1,0:T(8,128)S(1)}, f32[1024,32]{1,0:T(8,128)S(1)}, f32[1024,32]{1,0:T(8,128)S(1)}) fusion(f32[]{:T(128)} %get-tuple-element.338, pred[]{:T(512)} %get-tuple-element.337, s32[]{:T(128)} %get-tuple-element.336, s32[1024]{0:T(1024)S(1)} %iota_add_fusion.2, pred[1024]{0:T(1024)(128)(4,1)S(1)} %broadcast_compare_fusion.2), kind=kLoop, calls=%fused_computation.37.clone.1 | loop fusion | flops 458752 | bytes 398345 | tf_op jit(solution)/shard_map/while/body/neg | solution.py:63
  59.4 1.0 convolution_bitcast_fusion.2
  61.2 1.5 fusion.97
  63.9 1.0 cosine_select_fusion.4
  64.9 1.8 sine_select_fusion.4
  66.7 7.1 %fusion.96 = (f32[1024,32]{1,0:T(8,128)S(1)}, f32[1024,32]{1,0:T(8,128)S(1)}, f32[1024,32]{1,0:T(8,128)S(1)}) fusion(f32[]{:T(128)} %get-tuple-element.338, pred[]{:T(512)} %get-tuple-element.337, s32[]{:T(128)} %get-tuple-element.336, s32[1024]{0:T(1024)S(1)} %iota_add_fusion.2, pred[1024]{0:T(1024)(128)(4,1)S(1)} %broadcast_compare_fusion.2), kind=kLoop, calls=%fused_computation.37.clone.1 | loop fusion | flops 458752 | bytes 398345 | tf_op jit(solution)/shard_map/while/body/neg | solution.py:63
  73.8 1.0 convolution_bitcast_fusion.2
  75.5 1.5 fusion.97
  77.9 1.3 gather_fusion
  80.0 1.5 reduce.4
  82.3 174.3 %all-to-all-start.1 = ((bf16[4,2,2048]{2,1,0:T(2,128)(2,1)}), bf16[4,2,2048]{2,1,0:T(2,128)(2,1)S(1)}, u32[]{:S(2)}, u32[]{:S(2)}) async-start(bf16[4,2,2048]{2,1,0:T(2,128)(2,1)} %reshape.295), calls=%async_computation.1 | async-start | bytes 65536 | tf_op jit(solution)/shard_map/all_to_all | solution.py:137
  256.6 5.6 %all-to-all-done.1 = bf16[4,2,2048]{2,1,0:T(2,128)(2,1)S(1)} async-done(((bf16[4,2,2048]{2,1,0:T(2,128)(2,1)}), bf16[4,2,2048]{2,1,0:T(2,128)(2,1)S(1)}, u32[]{:S(2)}, u32[]{:S(2)}) %all-to-all-start.1) | async-done | bytes 32800 | tf_op jit(solution)/shard_map/all_to_all | solution.py:137
  264.4 1.0 select_bitcast_fusion
  265.4 5.3 %copy.139 = f32[32,64,513]{2,1,0:T(8,128)} copy(f32[32,64,513]{2,0,1:T(8,128)S(1)} %select_bitcast_fusion) | data formatting | bytes 8404992 | tf_op jit(solution)/shard_map/jit(_where)/select_n | solution.py:146
  270.7 6.2 %reshape.262 = f32[2,16,32832]{2,1,0:T(8,128)} reshape(f32[32,64,513]{2,1,0:T(8,128)} %copy.139) | data formatting | bytes 8404992 | tf_op jit(solution)/shard_map/reshape | solution.py:148
  276.9 92.9 %all-reduce.3.cloned.1.call-done = f32[2,16,32832]{2,1,0:T(8,128)} async-done(((f32[2,16,32832]{2,1,0:T(8,128)}), f32[2,16,32832]{2,1,0:T(8,128)}) %all-reduce.3.cloned.1.call-update) | async-done | bytes 4202512 | tf_op jit(solution)/shard_map/psum | solution.py:147
  369.9 4.5 %copy.191 = f32[2,16,32832]{2,1,0:T(8,128)} copy(f32[2,16,32832]{2,1,0:T(8,128)} %all-reduce.3.cloned.1.call-done) | data formatting | bytes 8404992
  (98 shorter events, 13.6 us)
Async XLA Ops:
  6.5 24.0 %copy-start = (f32[1,4,16016]{2,1,0:T(4,128)S(1)}, f32[1,4,16016]{2,1,0:T(4,128)}, u32[]{:S(2)}) copy-start(f32[1,4,16016]{2,1,0:T(4,128)} %param.13) | copy-start | bytes 768772
  17.0 9.2 %copy-start.1 = (s32[512]{0:T(512)S(1)}, s32[512]{0:T(512)}, u32[]{:S(2)}) copy-start(s32[512]{0:T(512)} %param.10) | copy-start | bytes 6148
  17.0 9.2 %copy-start.2 = (s32[1,4]{1,0:T(1,128)S(1)}, s32[1,4]{1,0:T(1,128)}, u32[]{:S(2)}) copy-start(s32[1,4]{1,0:T(1,128)} %param.11) | copy-start | bytes 52
  17.0 11.7 %copy-start.3 = (f32[1,4]{1,0:T(1,128)S(1)}, f32[1,4]{1,0:T(1,128)}, u32[]{:S(2)}) copy-start(f32[1,4]{1,0:T(1,128)} %param.12) | copy-start | bytes 52
  19.9 12.0 %all-to-all-start = ((bf16[4,128,32]{1,2,0:T(8,128)(2,1)}), bf16[4,128,32]{1,2,0:T(8,128)(2,1)S(1)}, u32[]{:S(2)}, u32[]{:S(2)}) async-start(bf16[4,128,32]{1,2,0:T(8,128)(2,1)} %copy.125), calls=%async_computation | async-start | bytes 65536 | tf_op jit(solution)/shard_map/all_to_all | solution.py:130
  82.3 180.0 %all-to-all-start.1 = ((bf16[4,2,2048]{2,1,0:T(2,128)(2,1)}), bf16[4,2,2048]{2,1,0:T(2,128)(2,1)S(1)}, u32[]{:S(2)}, u32[]{:S(2)}) async-start(bf16[4,2,2048]{2,1,0:T(2,128)(2,1)} %reshape.295), calls=%async_computation.1 | async-start | bytes 65536 | tf_op jit(solution)/shard_map/all_to_all | solution.py:137
  256.6 113.3 %all-reduce.3.cloned.1.call-start = ((), (), s32[]{:S(2)}) async-start(), calls=%async_computation.2 | async-start | bytes 8421376 | tf_op jit(solution)/shard_map/psum | solution.py:147
Sparse Core Ops, SparseCore 0:
  277.1 92.7 all-reduce.2
where the time goes:
time: 383 us; the launch traced here: 381 us
  starting transfers between devices  181 us (47%)
  waiting for transfers between devices  99.7 us (26%)
  local copies, waits for them, and re-layouts  35.2 us (9%)
  other arithmetic  35.2 us (9%)
  between operations  16.7 us (4%)
  matrix products  13.1 us (3%)
    all_to_all x1, starting transfers between devices, on_device(): lax.all_to_all(back[None], 'wave', split_axis=1, concat_axis=0, tiled=True)  174 us
    psum x1, waiting for transfers between devices, on_device(): total = lax.psum(partial_value, 'lat')  92.9 us
    neg x3, other arithmetic, analyse(): -inner_sin.T  21.2 us
  transfers between devices with their start and end apart: 3, of which 3 were waited for; matrix products, arithmetic and copies ran while one was open for 0% of the time, Pallas kernels for 0%

commit v1 on v0

v1 whole, which is shorter than its diff:
```python
import functools
import math

import jax
import jax.numpy as jnp
from jax import lax
from jax.experimental import pallas as pl
from jax.experimental.pallas import tpu as pltpu
from jax.sharding import PartitionSpec as P

TRUNC = 3999
M0 = 3488
MS = 512

F32 = jnp.float32
BF16 = jnp.bfloat16
RADIX = 4
CHUNK = 512


def dot(a, b, ca, cb):
    return lax.dot_general(a, b, (((ca,), (cb,)), ((), ())), preferred_element_type=F32)


def column_bounds(waves, first_slot, span):
    slot = first_slot + lax.broadcasted_iota(jnp.int32, waves.shape, 0)
    pair = slot // 2
    length = TRUNC + 1 - waves
    low = slot % 2 == 0
    begin = jnp.where(low, pair * span, (pair + 1) * span - length)
    end = jnp.where(low, pair * span + length, (pair + 1) * span)
    return begin, end


def fourier_kernel(span, waves_ref, spec_ref, leg_ref, out_ref):
    group, own = leg_ref.shape
    slots = waves_ref.shape[0]
    for first in range(0, slots, 8):
        c0 = first // 2 * span // 128 * 128
        c1 = min(-(-((first // 2 + 4) * span) // 128) * 128, own)
        begin, end = column_bounds(waves_ref[first : first + 8, :], first, span)
        column = c0 + lax.broadcasted_iota(jnp.int32, (8, c1 - c0), 1)
        inside = (column >= begin) & (column < end)
        rows = leg_ref[:, c0:c1].astype(F32)
        masked = jnp.concatenate(
            [jnp.where(inside, rows[r : r + 1, :], 0.0) for r in range(group)], 0
        ).astype(BF16)
        sums = dot(masked, spec_ref[:, c0:c1], 1, 1)
        for r in range(group):
            out_ref[r, first : first + 8, :] = sums[8 * r : 8 * r + 8, :].astype(BF16)


def output_kernel(span, waves_ref, leg_ref, back_ref, out_ref):
    rows, own = leg_ref.shape
    slots = waves_ref.shape[0]
    pairs = slots // 2
    for c0 in range(0, own, CHUNK):
        c1 = min(c0 + CHUNK, own)
        p0, p1 = c0 // span, (c1 - 1) // span + 1
        column = c0 + lax.broadcasted_iota(jnp.int32, (1, c1 - c0), 1)
        part = leg_ref[:, c0:c1].astype(F32)
        masked = []
        for pair in range(p0, p1):
            split = pair * span + TRUNC + 1 - waves_ref[2 * pair : 2 * pair + 1, :]
            low = (column >= pair * span) & (column < split)
            high = (column >= split) & (column < (pair + 1) * span)
            masked.append(jnp.where(low, part, 0.0))
            masked.append(jnp.where(high, part, 0.0))
        right = jnp.concatenate(masked, 0).astype(BF16)
        out_ref[:, c0:c1] = dot(back_ref[2 * p0 * rows : 2 * p1 * rows, :], right, 0, 0)


def sine_turns(v):
    y = v * v
    total = jnp.full_like(v, -((2 * math.pi) ** 11) / math.factorial(11))
    for power in (9, 7, 5, 3, 1):
        sign = 1.0 if power % 4 == 1 else -1.0
        total = total * y + sign * (2 * math.pi) ** power / math.factorial(power)
    return total * v


def angle_rows(count, start, width):
    row = lax.broadcasted_iota(jnp.int32, (32, width), 0)
    k = start + lax.broadcasted_iota(jnp.int32, (32, width), 1)
    mult = jnp.where(row < 8, M0 + 64 * row, jnp.where(row < 24, 4 * (row - 8), row - 24))
    product = (mult * k).astype(F32)
    inverse = 1.0 / count
    rest = product - count * jnp.round(product * inverse)
    turn = rest * inverse
    size = jnp.abs(turn)
    folded = jnp.minimum(size, 0.5 - size)
    return sine_turns(0.25 - size), jnp.where(turn < 0, -1.0, 1.0) * sine_turns(folded)


def halves(x):
    high = x.astype(BF16)
    return high, (x - high.astype(F32)).astype(BF16)


def order_matrix(waves):
    each = MS // RADIX
    column = lax.broadcasted_iota(jnp.int32, (MS, MS), 1)
    wave = M0 + RADIX * (column % each) + column // each
    return (waves == wave).astype(F32).astype(BF16)


def transform_kernel(info_ref, waves_ref, coef_ref, factor_ref, out_ref, acc_ref):
    count = info_ref[0]
    scale = info_ref[1]
    quarter = count * 0.25
    levels = coef_ref.shape[1] // 2
    each = MS // RADIX
    order = order_matrix(waves_ref[...])
    ordered = dot(coef_ref[...], order, 0, 0)
    real = [ordered[:levels, each * c : each * (c + 1)] for c in range(RADIX)]
    imag = [ordered[levels:, each * c : each * (c + 1)] for c in range(RADIX)]
    left = jnp.concatenate(
        [jnp.concatenate([real[c], -imag[c]], 1) for c in range(RADIX)]
        + [jnp.concatenate([imag[c], real[c]], 1) for c in range(1, RADIX)],
        0,
    ).astype(BF16)
    acc_ref[...] = jnp.zeros_like(acc_ref)

    def step(index, carry):
        start = index * CHUNK
        cos, sin = angle_rows(count, start, CHUNK)
        cos_b, sin_b = cos[8:24], sin[8:24]
        table = jnp.concatenate(
            [cos[a : a + 1] * cos_b - sin[a : a + 1] * sin_b for a in range(8)]
            + [sin[a : a + 1] * cos_b + cos[a : a + 1] * sin_b for a in range(8)],
            0,
        )
        high, low = halves(table)
        mixed = dot(left, high, 1, 0) + dot(left, low, 1, 0)
        h = [mixed[levels * i : levels * (i + 1)] for i in range(7)]
        c1, c2, c3 = cos[25:26], cos[26:27], cos[27:28]
        s1, s2, s3 = sin[25:26], sin[26:27], sin[27:28]
        re1, im1 = h[1] * c1 - h[4] * s1, h[1] * s1 + h[4] * c1
        re2 = h[2] * c2 - h[5] * s2
        re3, im3 = h[3] * c3 - h[6] * s3, h[3] * s3 + h[6] * c3
        e, f, p, d = h[0] + re2, h[0] - re2, re1 + re3, im1 - im3
        k = (start + lax.broadcasted_iota(jnp.int32, (1, CHUNK), 1)).astype(F32)
        g = jnp.where(k < quarter, factor_ref[:, pl.ds(pl.multiple_of(start, CHUNK), CHUNK)], 0.0)
        q0, q1, q2, q3 = g[0:1] * (e + p), g[1:2] * (f - d), g[2:3] * (e - p), g[3:4] * (f + d)
        x, y = q0 - q2, q1 - q3
        u, v = q0 + q2, q1 + q3
        w = u - v
        turned = jnp.concatenate(
            [
                u + v,
                x * c1 - y * s1,
                w * c2,
                x * c3 + y * s3,
                -(x * s1 + y * c1),
                -(w * s2),
                y * c3 - x * s3,
            ],
            0,
        )
        t_high, t_low = halves(turned)
        acc_ref[...] += dot(t_high, high, 1, 1) + dot(t_low, high, 1, 1) + dot(t_high, low, 1, 1)
        return carry

    lax.fori_loop(0, factor_ref.shape[1] // CHUNK, step, 0)
    total = acc_ref[...] * scale
    on_cos = [total[levels * i : levels * (i + 1), :each] for i in range(7)]
    on_sin = [total[levels * i : levels * (i + 1), each:] for i in range(7)]
    back_re = jnp.concatenate(
        [on_cos[0]] + [on_cos[c] + on_sin[c + 3] for c in range(1, RADIX)], 1
    )
    back_im = jnp.concatenate(
        [-on_sin[0]] + [on_cos[c + 3] - on_sin[c] for c in range(1, RADIX)], 1
    )
    back = jnp.concatenate([back_re, back_im], 0).astype(BF16)
    out_ref[...] = dot(order, back, 1, 1).astype(BF16)


PARAMS = pltpu.CompilerParams(vmem_limit_bytes=40 * 1024 * 1024)
VMEM = pl.BlockSpec(memory_space=pltpu.VMEM)
SMEM = pl.BlockSpec(memory_space=pltpu.SMEM)


def on_device(spectral, legendre, wave_of_slot, row_points, quad_weight, grid_factor):
    levels = spectral.shape[1]
    chans = 2 * levels
    owners = lax.axis_size("wave")
    groups = lax.axis_size("lat")
    per_owner = MS // owners
    group, own = legendre.shape
    span = own // (per_owner // 2)
    rows = groups * group
    gather = rows * legendre.dtype.itemsize < 2 * chans * 4
    me = lax.axis_index("wave")
    if gather:
        leg_all = lax.all_gather(legendre, "lat", axis=0, tiled=True)
    waves = wave_of_slot[:, None]
    mine = lax.dynamic_slice_in_dim(waves, me * per_owner, per_owner)
    coeffs = spectral.reshape(chans, own)
    fourier = pl.pallas_call(
        functools.partial(fourier_kernel, span),
        out_shape=jax.ShapeDtypeStruct((group, per_owner, chans), BF16),
        in_specs=[VMEM] * 3,
        out_specs=VMEM,
        compiler_params=PARAMS,
        name="fourier",
    )(mine, coeffs, legendre)
    arrived = lax.all_to_all(fourier, "wave", split_axis=0, concat_axis=1, tiled=True)[0]

    count = row_points[0, me]
    quarter = count // RADIX
    padded = -(-(grid_factor.shape[2] // RADIX) // CHUNK) * CHUNK
    row = jnp.pad(lax.dynamic_index_in_dim(grid_factor[0], me, 0, keepdims=False), (0, padded))
    factors = jnp.stack(
        [lax.dynamic_slice_in_dim(row, t * quarter, padded) for t in range(RADIX)]
    )
    points = count.astype(F32)
    info = jnp.stack([points, quad_weight[0, me] / points])
    back = pl.pallas_call(
        transform_kernel,
        out_shape=jax.ShapeDtypeStruct((MS, chans), BF16),
        in_specs=[SMEM] + [VMEM] * 3,
        out_specs=VMEM,
        scratch_shapes=[pltpu.VMEM((7 * levels, 2 * MS // RADIX), F32)],
        compiler_params=PARAMS,
        name="transform",
    )(info, waves, arrived, factors)
    returned = lax.all_to_all(back[None], "wave", split_axis=1, concat_axis=0, tiled=True)
    if gather:
        returned = lax.all_gather(returned, "lat", axis=0, tiled=True)
    table = leg_all if gather else legendre
    by_slot = returned.transpose(1, 0, 2).reshape(per_owner * table.shape[0], chans)
    out = pl.pallas_call(
        functools.partial(output_kernel, span),
        out_shape=jax.ShapeDtypeStruct((chans, own), F32),
        in_specs=[VMEM] * 3,
        out_specs=VMEM,
        compiler_params=PARAMS,
        name="output",
    )(mine, table, by_slot)
    if not gather:
        out = lax.psum(out, "lat")
    return out.reshape(2, levels, own)


def solution(mesh):
    return jax.shard_map(
        on_device,
        mesh=mesh,
        in_specs=(
            P(None, None, "wave"),
            P("lat", "wave"),
            P(),
            P("lat", None),
            P("lat", None),
            P("lat", None, None),
        ),
        out_specs=P(None, None, "wave"),
        check_vma=False,
    )
```

time: 383 us -> 69.2 us (0.18)
  starting transfers between devices: 181 us -> 6.35 us
  waiting for transfers between devices: 99.7 us -> 0.7 us
  other arithmetic: 35.2 us -> 1.64 us
  local copies, waits for them, and re-layouts: 35.2 us -> 11.4 us
  blocking collectives: 0 us -> 19.9 us
  matrix products: 13.1 us -> 0 us
  Pallas kernels: 0 us -> 11.4 us
    all_to_all x2 -> x1, starting transfers between devices: 181 us -> 6.31 us  [on_device(): lax.all_to_all(fourier, 'wave', split_axis=0, concat_axis=1, tiled=True)[0]]
    psum x1 -> x0, waiting for transfers between devices: 92.9 us -> none  [on_device(): total = lax.psum(partial_value, 'lat')]
    neg x6 -> x0, other arithmetic: 21.2 us -> none  [the longest x3 21.2 us: analyse(): -inner_sin.T]
    reshape x12 -> x0, local copies, waits for them, and re-layouts: 14.7 us -> none  [the longest x1 6.22 us: on_device(): return total.reshape(2, levels, own)]
    dot_general x10 -> x0, matrix products: 13.1 us -> none  [the longest x3 4.51 us: analyse(): jnp.dot(left, right, precision=lax.Precision.HIGH, preferred_element_type...]
    pallas_call x0 -> x3, Pallas kernels: none -> 11.4 us  [the longest x1 7.18 us: on_device(): pl.pallas_call(transform_kernel, out_shape=jax.ShapeDtypeStruct((MS, chan...]
    all_to_all x0 -> x1, blocking collectives: none -> 10.5 us  [on_device(): lax.all_to_all(back[None], 'wave', split_axis=1, concat_axis=0, tiled=True)]
    all_gather x0 -> x1, blocking collectives: none -> 9.32 us  [on_device(): returned = lax.all_gather(returned, 'lat', axis=0, tiled=True)]
  transfers between devices with their start and end apart: 3 -> 2, of which waited for: 3 -> 0; matrix products, arithmetic and copies ran while one was open for 0% -> 11% of each run, Pallas kernels for 0% -> 12%
where the time goes in v1:
time: 69.2 us; the launch traced here: 68.7 us
  blocking collectives  19.9 us (29%)
  between operations  17.4 us (25%)
  local copies, waits for them, and re-layouts  11.4 us (16%)
  Pallas kernels  11.4 us (16%)
  starting transfers between devices  6.35 us (9%)
  other arithmetic  1.64 us (2%)
  waiting for transfers between devices  0.7 us (1%)
    all_to_all x1, blocking collectives, on_device(): lax.all_to_all(back[None], 'wave', split_axis=1, concat_axis=0, tiled=True)  10.5 us
    all_gather x1, blocking collectives, on_device(): returned = lax.all_gather(returned, 'lat', axis=0, tiled=True)  9.32 us
    pallas_call x1, Pallas kernels, on_device(): pl.pallas_call(transform_kernel, out_shape=jax.ShapeDtypeStruct((MS, chan...  7.18 us
    all_to_all x1, starting transfers between devices, on_device(): lax.all_to_all(fourier, 'wave', split_axis=0, concat_axis=1, tiled=True)[0]  6.31 us
    unnamed x16, local copies, waits for them, and re-layouts  6.16 us
    pallas_call x1, Pallas kernels, on_device(): pl.pallas_call(functools.partial(output_kernel, span), out_shape=jax.Shap...  3.35 us
    unnamed x1, other arithmetic  1.5 us
    transpose x1, local copies, waits for them, and re-layouts, on_device(): returned.transpose(1, 0, 2).reshape(per_owner * table.shape[0], chans)  1.45 us
  transfers between devices with their start and end apart: 2, of which 0 were waited for; matrix products, arithmetic and copies ran while one was open for 11% of the time, Pallas kernels for 12%

profile of v1, /device:TPU:0, one launch (start us, length us, event | category | flops | bytes accessed | tf_op | source)
XLA Modules:
  0.0 68.7 jit_solution(3856009762504966177)
XLA Ops:
  6.5 0.0 all-gather.3.cloned.1.call-start
  6.6 0.7 all-gather.3.cloned.1.call-update
  7.3 0.8 %dynamic-slice_bitcast_fusion.1 = s32[128,1]{0,1:T(1,128)S(1)} fusion(s32[512]{0:T(512)} %param.8, s32[]{:T(128)S(6)} %select_n.23), kind=kLoop, calls=%fused_computation.9 | loop fusion | bytes 1028 | tf_op jit(solution)/shard_map/dynamic_slice | solution.py:197
  8.0 0.1 copy.30.waves_ref
  8.2 1.6 %copy-done.1 = bf16[2,16,32832]{2,1,0:T(8,128)(2,1)S(1)} copy-done((bf16[2,16,32832]{2,1,0:T(8,128)(2,1)S(1)}, bf16[2,16,32832]{2,1,0:T(8,128)(2,1)}, u32[]{:S(2)}) %copy-start.1) | copy-done | bytes 2101272
  9.7 0.9 %copy-done.2 = bf16[4,32832]{1,0:T(4,128)(2,1)S(1)} copy-done((bf16[4,32832]{1,0:T(4,128)(2,1)S(1)}, bf16[4,32832]{1,0:T(4,128)(2,1)}, u32[]{:S(2)}) %copy-start.2) | copy-done | bytes 262680
  10.7 0.8 %fourier.1 = bf16[4,128,32]{2,1,0:T(8,128)(2,1)S(1)} custom-call(s32[128,1]{1,0:T(8,128)S(1)} %copy.30.waves_ref, bf16[32,32832]{1,0:T(8,128)(2,1)S(1)} %bitcast.26, bf16[4,32832]{1,0:T(4,128)(2,1)S(1)} %copy-done.2), custom_call_target="tpu_custom_call" | custom-call | tf_op jit(solution)/shard_map/fourier/pallas_call | solution.py:199
  11.6 0.7 %copy.23 = bf16[4,128,32]{1,2,0:T(8,128)(2,1)} copy(bf16[4,128,32]{2,1,0:T(8,128)(2,1)S(1)} %fourier.1) | data formatting | bytes 65536 | tf_op jit(solution)/shard_map/fourier/pallas_call | solution.py:199
  12.3 6.3 %all-to-all-start = ((bf16[4,128,32]{1,2,0:T(8,128)(2,1)}), bf16[4,128,32]{1,2,0:T(8,128)(2,1)S(1)}, u32[]{:S(2)}, u32[]{:S(2)}) async-start(bf16[4,128,32]{1,2,0:T(8,128)(2,1)} %copy.23), calls=%async_computation | async-start | bytes 65536 | tf_op jit(solution)/shard_map/all_to_all | solution.py:207
  18.6 0.6 constant_dynamic-slice_fusion.1
  22.4 0.0 copy-done.5
  22.4 0.6 constant_dynamic-slice_fusion
  23.7 0.2 dynamic-slice_reduce_fusion
  23.9 0.1 pad_dynamic-slice_fusion.2
  24.0 0.1 pad_maximum_fusion.factor_ref
  24.1 0.1 pad_maximum_fusion.1.info_ref
  24.2 0.2 copy.25.waves_ref
  24.4 0.0 all-to-all-done
  24.4 0.1 copy.24
  24.5 7.2 %transform.1 = bf16[512,32]{1,0:T(8,128)(2,1)S(1)} custom-call(f32[2]{0:T(128)S(1)} %pad_maximum_fusion.1.info_ref, s32[512,1]{1,0:T(8,128)S(1)} %copy.25.waves_ref, bf16[512,32]{1,0:T(8,128)(2,1)S(1)} %bitcast.28, f32[4,4096]{1,0:T(4,128)S(1)} %pad_maximum_fusion.factor_ref), custom_call_target="tpu_custom_call" | custom-call | tf_op jit(solution)/shard_map/transform/pallas_call | solution.py:218
  31.7 0.2 copy.32
  31.9 0.5 broadcast.4
  32.4 1.5 %reduce.2 = bf16[512,32]{1,0:T(8,128)(2,1)S(1)} reduce(bf16[512,1,32]{2,1,0:T(2,128)(2,1)S(1)} %bitcast.31, bf16[]{:T(256)} %broadcast.4), dimensions={1}, to_apply=%bitcast.24.reduce_sub_computation | reduce | bytes 65538
  33.9 0.2 reshape.27
  34.1 10.5 %all_to_all.21 = bf16[4,2,2048]{2,1,0:T(2,128)(2,1)S(1)} all-to-all(bf16[4,2,2048]{2,1,0:T(2,128)(2,1)S(1)} %reshape.27), channel_id=1, replica_groups=mesh['wave'=4,'lat'=8] {'wave'}, dimensions={0} | all-to-all | bytes 65536 | tf_op jit(solution)/shard_map/all_to_all | solution.py:227
  44.6 0.2 reshape.28
  44.8 0.1 copy.27
  44.9 9.3 %all_gather.7 = bf16[32,128,32]{1,2,0:T(8,128)(2,1)S(1)} all-gather(bf16[4,128,32]{1,2,0:T(8,128)(2,1)S(1)} %copy.28), channel_id=1, replica_groups=mesh['wave'=4,'lat'=8] {'lat'}, dimensions={0}, use_global_device_ids=true | all-gather | bytes 294912 | tf_op jit(solution)/shard_map/all_gather | solution.py:229
  54.3 1.4 %copy.29 = bf16[128,32,32]{2,1,0:T(8,128)(2,1)S(1)} copy(bf16[128,32,32]{0,2,1:T(8,128)(2,1)S(1)} %bitcast.30) | data formatting | bytes 524288 | tf_op jit(solution)/shard_map/transpose | solution.py:231
  55.7 0.0 all-gather.3.cloned.1.call-done
  55.8 2.8 %reshape.25.leg_ref = bf16[32,32832]{1,0:T(8,128)(2,1)S(1)} reshape(bf16[8,4,32832]{2,1,0:T(4,128)(2,1)} %all-gather.3.cloned.1.call-done) | data formatting | bytes 4202496
  58.5 3.3 %output.1 = f32[32,32832]{1,0:T(8,128)} custom-call(s32[128,1]{1,0:T(8,128)S(1)} %copy.30.waves_ref, bf16[32,32832]{1,0:T(8,128)(2,1)S(1)} %reshape.25.leg_ref, bf16[4096,32]{1,0:T(8,128)(2,1)S(1)} %bitcast.25), custom_call_target="tpu_custom_call" | custom-call | tf_op jit(solution)/shard_map/output/pallas_call | solution.py:232
  (12 shorter events, 0.1 us)
Async XLA Ops:
  6.5 17.2 %copy-start = (f32[1,4,16016]{2,1,0:T(4,128)S(1)}, f32[1,4,16016]{2,1,0:T(4,128)}, u32[]{:S(2)}) copy-start(f32[1,4,16016]{2,1,0:T(4,128)} %param.11) | copy-start | bytes 768772
  6.5 17.7 %copy-start.3 = (s32[512]{0:T(512)S(1)}, s32[512]{0:T(512)}, u32[]{:S(2)}) copy-start(s32[512]{0:T(512)} %param.8) | copy-start | bytes 6148
  6.5 12.0 %copy-start.4 = (s32[1,4]{1,0:T(1,128)S(1)}, s32[1,4]{1,0:T(1,128)}, u32[]{:S(2)}) copy-start(s32[1,4]{1,0:T(1,128)} %param.9) | copy-start | bytes 52
  6.5 15.9 %copy-start.5 = (f32[1,4]{1,0:T(1,128)S(1)}, f32[1,4]{1,0:T(1,128)}, u32[]{:S(2)}) copy-start(f32[1,4]{1,0:T(1,128)} %param.10) | copy-start | bytes 52
  6.5 49.2 %all-gather.3.cloned.1.call-start = ((), (), s32[]{:S(2)}) async-start(), calls=%async_computation.2 | async-start | bytes 2368512 | tf_op jit(solution)/shard_map/all_gather | solution.py:195
  8.2 1.6 %copy-start.1 = (bf16[2,16,32832]{2,1,0:T(8,128)(2,1)S(1)}, bf16[2,16,32832]{2,1,0:T(8,128)(2,1)}, u32[]{:S(2)}) copy-start(bf16[2,16,32832]{2,1,0:T(8,128)(2,1)} %param.6) | copy-start | bytes 6303748
  9.7 1.0 %copy-start.2 = (bf16[4,32832]{1,0:T(4,128)(2,1)S(1)}, bf16[4,32832]{1,0:T(4,128)(2,1)}, u32[]{:S(2)}) copy-start(bf16[4,32832]{1,0:T(4,128)(2,1)} %leg_ref.1) | copy-start | bytes 787972
  12.3 12.1 %all-to-all-start = ((bf16[4,128,32]{1,2,0:T(8,128)(2,1)}), bf16[4,128,32]{1,2,0:T(8,128)(2,1)S(1)}, u32[]{:S(2)}, u32[]{:S(2)}) async-start(bf16[4,128,32]{1,2,0:T(8,128)(2,1)} %copy.23), calls=%async_computation | async-start | bytes 65536 | tf_op jit(solution)/shard_map/all_to_all | solution.py:207
Sparse Core Ops, SparseCore 0:
  9.3 30.6 all-gather.2

commit v2 on v1

v2 whole, which is shorter than its diff:
```python
import functools
import math

import jax
import jax.numpy as jnp
from jax import lax
from jax.experimental import pallas as pl
from jax.experimental.pallas import tpu as pltpu
from jax.sharding import PartitionSpec as P

TRUNC = 3999
M0 = 3488
MS = 512

F32 = jnp.float32
BF16 = jnp.bfloat16
MESH = pl.DeviceIdType.MESH
RADIX = 4
CHUNK = 512


def dot(a, b, ca, cb):
    return lax.dot_general(a, b, (((ca,), (cb,)), ((), ())), preferred_element_type=F32)


def column_bounds(waves, first_slot, span):
    slot = first_slot + lax.broadcasted_iota(jnp.int32, waves.shape, 0)
    pair = slot // 2
    length = TRUNC + 1 - waves
    low = slot % 2 == 0
    begin = jnp.where(low, pair * span, (pair + 1) * span - length)
    end = jnp.where(low, pair * span + length, (pair + 1) * span)
    return begin, end


def prepare_kernel(span, points_ref, waves_ref, spec_ref, leg_ref, grid_ref, out_ref, factor_ref, acc_ref, row_ref):
    me = lax.axis_index("wave")
    group, own = leg_ref.shape
    slots = acc_ref.shape[1]
    for first in range(0, slots, 8):
        c0 = first // 2 * span // 128 * 128
        c1 = min(-(-((first // 2 + 4) * span) // 128) * 128, own)
        waves = waves_ref[pl.ds(pl.multiple_of(me * slots + first, 8), 8), :]
        begin, end = column_bounds(waves, first, span)
        column = c0 + lax.broadcasted_iota(jnp.int32, (8, c1 - c0), 1)
        inside = (column >= begin) & (column < end)
        rows = leg_ref[:, c0:c1].astype(F32)
        masked = jnp.concatenate(
            [jnp.where(inside, rows[r : r + 1, :], 0.0) for r in range(group)], 0
        ).astype(BF16)
        sums = dot(masked, spec_ref[:, c0:c1], 1, 1)
        for r in range(group):
            acc_ref[r, first : first + 8, :] = sums[8 * r : 8 * r + 8, :]
    for r in range(group):
        out_ref[r] = acc_ref[r].T.astype(BF16)
    wide = row_ref.shape[1]
    row_ref[...] = jnp.zeros_like(row_ref)
    row_ref[:, : grid_ref.shape[1]] = grid_ref[pl.ds(me, 1), :]
    row = row_ref[...]
    quarter = points_ref[0, me] // RADIX
    for t in range(RADIX):
        shifted = pltpu.roll(row, wide - t * quarter, 1) if t else row
        factor_ref[t : t + 1, :] = shifted[:, : factor_ref.shape[1]]


def output_kernel(span, waves_ref, leg_ref, back_ref, out_ref, held_ref):
    me = lax.axis_index("wave")
    groups, group, own = leg_ref.shape
    rows, _, slots = back_ref.shape
    for r in range(rows):
        held_ref[slots * r : slots * (r + 1), :] = back_ref[r].astype(F32).T
    for c0 in range(0, own, CHUNK):
        c1 = min(c0 + CHUNK, own)
        p0, p1 = c0 // span, (c1 - 1) // span + 1
        column = c0 + lax.broadcasted_iota(jnp.int32, (1, c1 - c0), 1)
        part = jnp.concatenate([leg_ref[g, :, c0:c1].astype(F32) for g in range(groups)], 0)
        masked, left = [], []
        for pair in range(p0, p1):
            split = pair * span + TRUNC + 1 - waves_ref[me * slots + 2 * pair]
            low = (column >= pair * span) & (column < split)
            high = (column >= split) & (column < (pair + 1) * span)
            masked.append(jnp.where(low, part, 0.0))
            masked.append(jnp.where(high, part, 0.0))
            left.append(held_ref[pl.ds(2 * pair, rows, stride=slots), :])
            left.append(held_ref[pl.ds(2 * pair + 1, rows, stride=slots), :])
        right = jnp.concatenate(masked, 0).astype(BF16)
        out_ref[:, c0:c1] = dot(jnp.concatenate(left, 0).astype(BF16), right, 0, 0)


def sine_turns(v):
    y = v * v
    total = jnp.full_like(v, -((2 * math.pi) ** 11) / math.factorial(11))
    for power in (9, 7, 5, 3, 1):
        sign = 1.0 if power % 4 == 1 else -1.0
        total = total * y + sign * (2 * math.pi) ** power / math.factorial(power)
    return total * v


def angle_rows(count, start, width):
    row = lax.broadcasted_iota(jnp.int32, (32, width), 0)
    k = start + lax.broadcasted_iota(jnp.int32, (32, width), 1)
    mult = jnp.where(row < 8, M0 + 64 * row, jnp.where(row < 24, 4 * (row - 8), row - 24))
    product = (mult * k).astype(F32)
    inverse = 1.0 / count
    rest = product - count * jnp.round(product * inverse)
    turn = rest * inverse
    size = jnp.abs(turn)
    folded = jnp.minimum(size, 0.5 - size)
    return sine_turns(0.25 - size), jnp.where(turn < 0, -1.0, 1.0) * sine_turns(folded)


def halves(x):
    high = x.astype(BF16)
    return high, (x - high.astype(F32)).astype(BF16)


def order_matrix(waves):
    each = MS // RADIX
    column = lax.broadcasted_iota(jnp.int32, (MS, MS), 1)
    wave = M0 + RADIX * (column % each) + column // each
    return (waves == wave).astype(F32).astype(BF16)


def transform_kernel(
    owners, groups, points_ref, weight_ref, waves_ref, four_ref, factor_ref,
    out_ref, came_ref, leave_ref, acc_ref, high_ref, low_ref, turn_ref,
    send_four, recv_four, send_back, recv_back,
):
    me, here = lax.axis_index("wave"), lax.axis_index("lat")
    lats = lax.axis_size("lat")
    base = here * owners if groups > 1 else 0
    offsets = [(w, l) for l in range(groups) for w in range(owners) if w or l]

    def peer(offset):
        return lax.rem(me + offset[0], owners), lax.rem(here + offset[1], lats)

    barrier = pltpu.get_barrier_semaphore()
    for offset in offsets:
        pl.semaphore_signal(barrier, inc=1, device_id=peer(offset), device_id_type=MESH)
    pl.semaphore_wait(barrier, len(offsets))

    def four_copy(step, to, owner):
        return pltpu.make_async_remote_copy(
            src_ref=four_ref.at[to],
            dst_ref=came_ref.at[owner],
            send_sem=send_four.at[step],
            recv_sem=recv_four.at[owner],
            device_id=(to, here),
            device_id_type=MESH,
        )

    for step in range(1, owners):
        four_copy(step, lax.rem(me + step, owners), me).start()
    came_ref[me] = four_ref[me]

    count = points_ref[0, me].astype(F32)
    scale = weight_ref[0, me] / count
    quarter = count * 0.25
    levels = four_ref.shape[1] // 2
    each = MS // RADIX
    order = order_matrix(waves_ref[...])

    def make_tables(index, carry):
        start = index * CHUNK
        cos, sin = angle_rows(count, start, CHUNK)
        cos_b, sin_b = cos[8:24], sin[8:24]
        table = jnp.concatenate(
            [cos[a : a + 1] * cos_b - sin[a : a + 1] * sin_b for a in range(8)]
            + [sin[a : a + 1] * cos_b + cos[a : a + 1] * sin_b for a in range(8)],
            0,
        )
        high, low = halves(table)
        high_ref[index] = high
        low_ref[index] = low
        turn_ref[index, :8] = cos[24:32]
        turn_ref[index, 8:] = sin[24:32]
        return carry

    chunks = factor_ref.shape[1] // CHUNK
    lax.fori_loop(0, chunks, make_tables, 0)
    acc_ref[...] = jnp.zeros_like(acc_ref)

    for step in range(1, owners):
        four_copy(step, lax.rem(me + step, owners), me).wait_send()
        owner = lax.rem(me + owners - step, owners)
        four_copy(step, owner, owner).wait_recv()
    arrived = jnp.concatenate([came_ref[w] for w in range(owners)], 1)
    ordered = dot(arrived, order, 1, 0)
    real = [ordered[:levels, each * c : each * (c + 1)] for c in range(RADIX)]
    imag = [ordered[levels:, each * c : each * (c + 1)] for c in range(RADIX)]
    left = jnp.concatenate(
        [jnp.concatenate([real[c], -imag[c]], 1) for c in range(RADIX)]
        + [jnp.concatenate([imag[c], real[c]], 1) for c in range(1, RADIX)],
        0,
    ).astype(BF16)

    def step(index, carry):
        start = index * CHUNK
        high, low = high_ref[index], low_ref[index]
        turns = turn_ref[index]
        mixed = dot(left, high, 1, 0) + dot(left, low, 1, 0)
        h = [mixed[levels * i : levels * (i + 1)] for i in range(7)]
        c1, c2, c3 = turns[1:2], turns[2:3], turns[3:4]
        s1, s2, s3 = turns[9:10], turns[10:11], turns[11:12]
        re1, im1 = h[1] * c1 - h[4] * s1, h[1] * s1 + h[4] * c1
        re2 = h[2] * c2 - h[5] * s2
        re3, im3 = h[3] * c3 - h[6] * s3, h[3] * s3 + h[6] * c3
        e, f, p, d = h[0] + re2, h[0] - re2, re1 + re3, im1 - im3
        k = (start + lax.broadcasted_iota(jnp.int32, (1, CHUNK), 1)).astype(F32)
        g = jnp.where(k < quarter, factor_ref[:, pl.ds(pl.multiple_of(start, CHUNK), CHUNK)], 0.0)
        q0, q1, q2, q3 = g[0:1] * (e + p), g[1:2] * (f - d), g[2:3] * (e - p), g[3:4] * (f + d)
        x, y = q0 - q2, q1 - q3
        u, v = q0 + q2, q1 + q3
        w = u - v
        turned = jnp.concatenate(
            [
                u + v,
                x * c1 - y * s1,
                w * c2,
                x * c3 + y * s3,
                -(x * s1 + y * c1),
                -(w * s2),
                y * c3 - x * s3,
            ],
            0,
        )
        t_high, t_low = halves(turned)
        acc_ref[...] += dot(t_high, high, 1, 1) + dot(t_low, high, 1, 1) + dot(t_high, low, 1, 1)
        return carry

    lax.fori_loop(0, chunks, step, 0)
    total = acc_ref[...] * scale
    on_cos = [total[levels * i : levels * (i + 1), :each] for i in range(7)]
    on_sin = [total[levels * i : levels * (i + 1), each:] for i in range(7)]
    back_re = jnp.concatenate(
        [on_cos[0]] + [on_cos[c] + on_sin[c + 3] for c in range(1, RADIX)], 1
    )
    back_im = jnp.concatenate(
        [-on_sin[0]] + [on_cos[c + 3] - on_sin[c] for c in range(1, RADIX)], 1
    )
    back = jnp.concatenate([back_re, back_im], 0).astype(BF16)
    by_slot = dot(back, order, 1, 1).astype(BF16)
    slots = four_ref.shape[2]
    for w in range(owners):
        leave_ref[w] = by_slot[:, slots * w : slots * (w + 1)]

    def back_copy(step, to, row):
        return pltpu.make_async_remote_copy(
            src_ref=leave_ref.at[to[0]],
            dst_ref=out_ref.at[row],
            send_sem=send_back.at[step],
            recv_sem=recv_back.at[row],
            device_id=to,
            device_id_type=MESH,
        )

    for step, offset in enumerate(offsets):
        back_copy(step, peer(offset), base + me).start()
    out_ref[base + me] = leave_ref[me]
    for step, offset in enumerate(offsets):
        back_copy(step, peer(offset), base + me).wait_send()
        source = lax.rem(me + owners - offset[0], owners), lax.rem(here + lats - offset[1], lats)
        row = source[1] * owners + source[0] if groups > 1 else source[0]
        back_copy(step, source, row).wait_recv()


PARAMS = pltpu.CompilerParams(vmem_limit_bytes=40 * 1024 * 1024)
VMEM = pl.BlockSpec(memory_space=pltpu.VMEM)
SMEM = pl.BlockSpec(memory_space=pltpu.SMEM)


def on_device(spectral, legendre, wave_of_slot, row_points, quad_weight, grid_factor):
    levels = spectral.shape[1]
    chans = 2 * levels
    owners = lax.axis_size("wave")
    groups = lax.axis_size("lat")
    per_owner = MS // owners
    group, own = legendre.shape
    span = own // (per_owner // 2)
    gather = groups * group * legendre.dtype.itemsize < 2 * chans * 4
    table = lax.all_gather(legendre, "lat") if gather else legendre[None]
    waves = wave_of_slot[:, None]
    coeffs = spectral.reshape(chans, own)
    length = grid_factor.shape[2]
    padded = -(-(length // RADIX) // CHUNK) * CHUNK
    wide = -(-length // 128) * 128
    fourier, factors = pl.pallas_call(
        functools.partial(prepare_kernel, span),
        out_shape=[
            jax.ShapeDtypeStruct((group, chans, per_owner), BF16),
            jax.ShapeDtypeStruct((RADIX, padded), F32),
        ],
        in_specs=[SMEM] + [VMEM] * 4,
        out_specs=[VMEM] * 2,
        scratch_shapes=[pltpu.VMEM((group, per_owner, chans), F32), pltpu.VMEM((1, wide), F32)],
        compiler_params=PARAMS,
        name="prepare",
    )(row_points, waves, coeffs, legendre, grid_factor[0])
    used = groups if gather else 1
    others = owners * used - 1
    back = pl.pallas_call(
        functools.partial(transform_kernel, owners, used),
        out_shape=jax.ShapeDtypeStruct((owners * used, chans, per_owner), BF16),
        in_specs=[SMEM] * 2 + [VMEM] * 3,
        out_specs=VMEM,
        scratch_shapes=[
            pltpu.VMEM((owners, chans, per_owner), BF16),
            pltpu.VMEM((owners, chans, per_owner), BF16),
            pltpu.VMEM((7 * levels, 2 * MS // RADIX), F32),
            pltpu.VMEM((padded // CHUNK, 2 * MS // RADIX, CHUNK), BF16),
            pltpu.VMEM((padded // CHUNK, 2 * MS // RADIX, CHUNK), BF16),
            pltpu.VMEM((padded // CHUNK, 16, CHUNK), F32),
            pltpu.SemaphoreType.DMA((owners,)),
            pltpu.SemaphoreType.DMA((owners,)),
            pltpu.SemaphoreType.DMA((others,)),
            pltpu.SemaphoreType.DMA((owners * used,)),
        ],
        compiler_params=pltpu.CompilerParams(
            collective_id=0, has_side_effects=True, vmem_limit_bytes=40 * 1024 * 1024
        ),
        name="transform",
    )(row_points, quad_weight, waves, fourier, factors)
    out = pl.pallas_call(
        functools.partial(output_kernel, span),
        out_shape=jax.ShapeDtypeStruct((chans, own), F32),
        in_specs=[SMEM] + [VMEM] * 2,
        out_specs=VMEM,
        scratch_shapes=[pltpu.VMEM((owners * used * per_owner, chans), F32)],
        compiler_params=PARAMS,
        name="output",
    )(wave_of_slot, table, back)
    if not gather:
        out = lax.psum(out, "lat")
    return out.reshape(2, levels, own)


def solution(mesh):
    return jax.shard_map(
        on_device,
        mesh=mesh,
        in_specs=(
            P(None, None, "wave"),
            P("lat", "wave"),
            P(),
            P("lat", None),
            P("lat", None),
            P("lat", None, None),
        ),
        out_specs=P(None, None, "wave"),
        check_vma=False,
    )
```

time: 69.2 us -> 55.2 us (0.80)
  blocking collectives: 19.9 us -> 0 us
  Pallas kernels: 11.4 us -> 30.7 us
  starting transfers between devices: 6.35 us -> 0.01 us
  local copies, waits for them, and re-layouts: 11.4 us -> 6.56 us
  between operations: 17.4 us -> 13.4 us
  waiting for transfers between devices: 0.7 us -> 4.21 us
  other arithmetic: 1.64 us -> 0 us
    pallas_call x2, Pallas kernels: 8.03 us -> 25.5 us  [the longest x1 23.5 us: on_device(): pl.pallas_call(functools.partial(transform_kernel, owners, used), out_sha...]
    all_to_all x1 -> x0, blocking collectives: 10.5 us -> none  [on_device(): lax.all_to_all(back[None], 'wave', split_axis=1, concat_axis=0, tiled=True)]
    all_gather x1 -> x0, blocking collectives: 9.32 us -> none  [on_device(): returned = lax.all_gather(returned, 'lat', axis=0, tiled=True)]
    all_to_all x1 -> x0, starting transfers between devices: 6.31 us -> none  [on_device(): lax.all_to_all(fourier, 'wave', split_axis=0, concat_axis=1, tiled=True)[0]]
    all_gather x1, waiting for transfers between devices: 0.02 us -> 3.5 us  [on_device(): table = lax.all_gather(legendre, 'lat') if gather else legendre[None]]
    dynamic_slice x6 -> x0, local copies, waits for them, and re-layouts: 2.46 us -> none  [the longest x2 0.87 us: on_device(): mine = lax.dynamic_slice_in_dim(waves, me * per_owner, per_owner)]
    pallas_call x1, Pallas kernels: 3.35 us -> 5.22 us  [on_device(): pl.pallas_call(functools.partial(output_kernel, span), out_shape=jax.Shap...]
    unnamed x1 -> x0, other arithmetic: 1.5 us -> none
  transfers between devices with their start and end apart: 2 -> 1, of which waited for: 0 -> 1; matrix products, arithmetic and copies ran while one was open for 11% -> 1% of each run, Pallas kernels for 12% -> 46%
where the time goes in v2:
time: 55.2 us; the launch traced here: 54.9 us
  Pallas kernels  30.7 us (56%)
  between operations  13.4 us (24%)
  local copies, waits for them, and re-layouts  6.56 us (12%)
  waiting for transfers between devices  4.21 us (8%)
    pallas_call x1, Pallas kernels, on_device(): pl.pallas_call(functools.partial(transform_kernel, owners, used), out_sha...  23.5 us
    unnamed x14, local copies, waits for them, and re-layouts  5.74 us
    pallas_call x1, Pallas kernels, on_device(): pl.pallas_call(functools.partial(output_kernel, span), out_shape=jax.Shap...  5.22 us
    all_gather x1, waiting for transfers between devices, on_device(): table = lax.all_gather(legendre, 'lat') if gather else legendre[None]  3.5 us
    pallas_call x1, Pallas kernels, on_device(): pl.pallas_call(functools.partial(prepare_kernel, span), out_shape=[jax.Sh...  2 us
  transfers between devices with their start and end apart: 1, of which 1 were waited for; matrix products, arithmetic and copies ran while one was open for 1% of the time, Pallas kernels for 46%

profile of v2, /device:TPU:0, one launch (start us, length us, event | category | flops | bytes accessed | tf_op | source)
XLA Modules:
  0.0 54.9 jit_solution(18340930636741865409)
XLA Ops:
  6.5 0.0 copy-start.4
  6.5 0.0 copy-start.6
  6.5 0.0 all-gather.4.cloned.1.call-start
  6.5 0.7 %all-gather.4.cloned.1.call-update = ((bf16[1,4,32832]{2,1,0:T(4,128)(2,1)}), bf16[8,4,32832]{2,1,0:T(4,128)(2,1)}) async-update(((), (), s32[]{:S(2)}) %all-gather.4.cloned.1.call-start, bf16[1,4,32832]{2,1,0:T(4,128)(2,1)} %bitcast.6) | async-update | bytes 2626584
  7.3 0.8 %copy.10.waves_ref = s32[512,1]{1,0:T(8,128)S(1)} copy(s32[512,1]{0,1:T(1,128)} %bitcast.8) | data formatting | bytes 4096 | tf_op jit(solution)/shard_map/broadcast_in_dim | solution.py:282
  8.1 0.0 copy-start
  8.1 1.6 %copy-done = bf16[2,16,32832]{2,1,0:T(8,128)(2,1)S(1)} copy-done((bf16[2,16,32832]{2,1,0:T(8,128)(2,1)S(1)}, bf16[2,16,32832]{2,1,0:T(8,128)(2,1)}, u32[]{:S(2)}) %copy-start) | copy-done | bytes 2101272
  9.7 0.0 copy-start.2
  9.7 0.9 %copy-done.2 = bf16[4,32832]{1,0:T(4,128)(2,1)S(1)} copy-done((bf16[4,32832]{1,0:T(4,128)(2,1)S(1)}, bf16[4,32832]{1,0:T(4,128)(2,1)}, u32[]{:S(2)}) %copy-start.2) | copy-done | bytes 262680
  10.6 0.0 copy-start.3
  10.6 0.9 %copy-done.3 = f32[1,4,16016]{2,1,0:T(4,128)S(1)} copy-done((f32[1,4,16016]{2,1,0:T(4,128)S(1)}, f32[1,4,16016]{2,1,0:T(4,128)}, u32[]{:S(2)}) %copy-start.3) | copy-done | bytes 256280
  11.6 0.0 copy-start.5
  11.6 0.7 %copy-done.5 = s32[1,4]{1,0:T(1,128)S(1)} copy-done((s32[1,4]{1,0:T(1,128)S(1)}, s32[1,4]{1,0:T(1,128)}, u32[]{:S(2)}) %copy-start.5) | copy-done | bytes 40
  12.2 2.0 %prepare.1 = (bf16[4,32,128]{2,1,0:T(8,128)(2,1)S(1)}, f32[4,4096]{1,0:T(4,128)S(1)}) custom-call(s32[1,4]{1,0:T(1,128)S(1)} %copy-done.5, s32[512,1]{1,0:T(8,128)S(1)} %copy.10.waves_ref, bf16[32,32832]{1,0:T(8,128)(2,1)S(1)} %bitcast.5, bf16[4,32832]{1,0:T(4,128)(2,1)S(1)} %copy-done.2, f32[4,16016]{1,0:T(4,128)S(1)} %bitcast.7), custom_call_target="tpu_custom_call" | custom-call | tf_op jit(solution)/shard_map/prepare/pallas_call | solution.py:287
  14.2 0.0 copy-done.6
  14.3 23.5 %transform.1.back_ref = bf16[32,32,128]{2,1,0:T(8,128)(2,1)S(1)} custom-call(s32[1,4]{1,0:T(1,128)S(1)} %copy-done.5, f32[1,4]{1,0:T(1,128)S(1)} %copy-done.6, s32[512,1]{1,0:T(8,128)S(1)} %copy.10.waves_ref, bf16[4,32,128]{2,1,0:T(8,128)(2,1)S(1)} %get-tuple-element.7.four_ref, f32[4,4096]{1,0:T(4,128)S(1)} %get-tuple-element.8.factor_ref), custom_call_target="tpu_custom_call" | custom-call | tf_op jit(solution)/shard_map/transform/pallas_call | solution.py:301
  37.8 3.5 %all-gather.4.cloned.1.call-done.leg_ref = bf16[8,4,32832]{2,1,0:T(4,128)(2,1)} async-done(((bf16[1,4,32832]{2,1,0:T(4,128)(2,1)}), bf16[8,4,32832]{2,1,0:T(4,128)(2,1)}) %all-gather.4.cloned.1.call-update) | async-done | bytes 2101264 | tf_op jit(solution)/shard_map/all_gather | solution.py:281
  41.3 0.0 copy-done.4
  41.3 0.0 copy-start.1
  41.3 1.6 %copy-done.1 = bf16[8,4,32832]{2,1,0:T(4,128)(2,1)S(1)} copy-done((bf16[8,4,32832]{2,1,0:T(4,128)(2,1)S(1)}, bf16[8,4,32832]{2,1,0:T(4,128)(2,1)}, u32[]{:S(2)}) %copy-start.1) | copy-done | bytes 2101272
  42.9 5.2 %output.1 = f32[32,32832]{1,0:T(8,128)} custom-call(s32[512]{0:T(512)S(1)} %copy-done.4, bf16[8,4,32832]{2,1,0:T(4,128)(2,1)S(1)} %copy-done.1, bf16[32,32,128]{2,1,0:T(8,128)(2,1)S(1)} %transform.1.back_ref), custom_call_target="tpu_custom_call" | custom-call | tf_op jit(solution)/shard_map/output/pallas_call | solution.py:323
Async XLA Ops:
  6.5 34.7 %copy-start.4 = (s32[512]{0:T(512)S(1)}, s32[512]{0:T(512)}, u32[]{:S(2)}) copy-start(s32[512]{0:T(512)} %waves_ref.1) | copy-start | bytes 6148
  6.5 7.7 %copy-start.6 = (f32[1,4]{1,0:T(1,128)S(1)}, f32[1,4]{1,0:T(1,128)}, u32[]{:S(2)}) copy-start(f32[1,4]{1,0:T(1,128)} %weight_ref.1) | copy-start | bytes 52
  6.5 34.7 %all-gather.4.cloned.1.call-start = ((), (), s32[]{:S(2)}) async-start(), calls=%async_computation | async-start | bytes 2368512 | tf_op jit(solution)/shard_map/all_gather | solution.py:281
  8.1 1.6 %copy-start = (bf16[2,16,32832]{2,1,0:T(8,128)(2,1)S(1)}, bf16[2,16,32832]{2,1,0:T(8,128)(2,1)}, u32[]{:S(2)}) copy-start(bf16[2,16,32832]{2,1,0:T(8,128)(2,1)} %param.6) | copy-start | bytes 6303748
  9.7 1.0 %copy-start.2 = (bf16[4,32832]{1,0:T(4,128)(2,1)S(1)}, bf16[4,32832]{1,0:T(4,128)(2,1)}, u32[]{:S(2)}) copy-start(bf16[4,32832]{1,0:T(4,128)(2,1)} %leg_ref.1) | copy-start | bytes 787972
  10.6 0.9 %copy-start.3 = (f32[1,4,16016]{2,1,0:T(4,128)S(1)}, f32[1,4,16016]{2,1,0:T(4,128)}, u32[]{:S(2)}) copy-start(f32[1,4,16016]{2,1,0:T(4,128)} %param.11) | copy-start | bytes 768772
  11.6 0.7 %copy-start.5 = (s32[1,4]{1,0:T(1,128)S(1)}, s32[1,4]{1,0:T(1,128)}, u32[]{:S(2)}) copy-start(s32[1,4]{1,0:T(1,128)} %points_ref.3) | copy-start | bytes 52
  41.3 1.6 %copy-start.1 = (bf16[8,4,32832]{2,1,0:T(4,128)(2,1)S(1)}, bf16[8,4,32832]{2,1,0:T(4,128)(2,1)}, u32[]{:S(2)}) copy-start(bf16[8,4,32832]{2,1,0:T(4,128)(2,1)} %all-gather.4.cloned.1.call-done.leg_ref) | copy-start | bytes 6303748
Sparse Core Ops, SparseCore 0:
  9.2 31.9 all-gather.3

commit v3 on v2

--- a/solution.py
+++ b/solution.py
@@ -33,14 +33,42 @@
     return begin, end
 
 
-def prepare_kernel(span, points_ref, waves_ref, spec_ref, leg_ref, grid_ref, out_ref, factor_ref, acc_ref, row_ref):
+def wave_column(waves_ref):
+    row = waves_ref[...].astype(F32)
+    return jnp.broadcast_to(row, (8, row.shape[1])).T[:, :1]
+
+
+def prepare_kernel(
+    span, points_ref, waves_ref, spec_hbm, leg_hbm, grid_hbm, out_ref, factor_ref, packed_ref,
+    acc_ref, row_ref, column_ref, pack_ref, spec_ref, leg_ref, grid_ref, sems,
+):
     me = lax.axis_index("wave")
+    copies = [
+        pltpu.make_async_copy(source, target, sems.at[i])
+        for i, (source, target) in enumerate(
+            ((spec_hbm, spec_ref), (leg_hbm, leg_ref), (grid_hbm, grid_ref))
+        )
+    ]
+    for copy in copies:
+        copy.start()
+    column_ref[...] = wave_column(waves_ref).astype(jnp.int32)
+    for copy in copies:
+        copy.wait()
     group, own = leg_ref.shape
+    length = packed_ref.shape[1]
+    for piece in range(packed_ref.shape[0] // group):
+        first, last = piece * length, min((piece + 1) * length, own)
+        if last - first < length:
+            pack_ref[group * piece : group * (piece + 1), :] = jnp.zeros((group, length), F32)
+        pack_ref[group * piece : group * (piece + 1), : last - first] = leg_ref[
+            :, first:last
+        ].astype(F32)
+    packed_ref[...] = pack_ref[...].astype(BF16)
     slots = acc_ref.shape[1]
     for first in range(0, slots, 8):
         c0 = first // 2 * span // 128 * 128
         c1 = min(-(-((first // 2 + 4) * span) // 128) * 128, own)
-        waves = waves_ref[pl.ds(pl.multiple_of(me * slots + first, 8), 8), :]
+        waves = column_ref[pl.ds(pl.multiple_of(me * slots + first, 8), 8), :]
         begin, end = column_bounds(waves, first, span)
         column = c0 + lax.broadcasted_iota(jnp.int32, (8, c1 - c0), 1)
         inside = (column >= begin) & (column < end)
@@ -63,28 +91,36 @@
         factor_ref[t : t + 1, :] = shifted[:, : factor_ref.shape[1]]
 
 
-def output_kernel(span, waves_ref, leg_ref, back_ref, out_ref, held_ref):
+def output_kernel(span, group, waves_ref, leg_ref, back_ref, out_ref, held_ref):
     me = lax.axis_index("wave")
-    groups, group, own = leg_ref.shape
+    groups, packed, length = leg_ref.shape
+    own = out_ref.shape[1]
     rows, _, slots = back_ref.shape
     for r in range(rows):
         held_ref[slots * r : slots * (r + 1), :] = back_ref[r].astype(F32).T
-    for c0 in range(0, own, CHUNK):
-        c1 = min(c0 + CHUNK, own)
-        p0, p1 = c0 // span, (c1 - 1) // span + 1
-        column = c0 + lax.broadcasted_iota(jnp.int32, (1, c1 - c0), 1)
-        part = jnp.concatenate([leg_ref[g, :, c0:c1].astype(F32) for g in range(groups)], 0)
-        masked, left = [], []
-        for pair in range(p0, p1):
-            split = pair * span + TRUNC + 1 - waves_ref[me * slots + 2 * pair]
-            low = (column >= pair * span) & (column < split)
-            high = (column >= split) & (column < (pair + 1) * span)
-            masked.append(jnp.where(low, part, 0.0))
-            masked.append(jnp.where(high, part, 0.0))
-            left.append(held_ref[pl.ds(2 * pair, rows, stride=slots), :])
-            left.append(held_ref[pl.ds(2 * pair + 1, rows, stride=slots), :])
-        right = jnp.concatenate(masked, 0).astype(BF16)
-        out_ref[:, c0:c1] = dot(jnp.concatenate(left, 0).astype(BF16), right, 0, 0)
+    for at in range(0, length, CHUNK):
+        parts = [leg_ref[g, :, at : min(at + CHUNK, length)].astype(F32) for g in range(groups)]
+        for piece in range(packed // group):
+            c0 = piece * length + at
+            c1 = min(c0 + CHUNK, (piece + 1) * length, own)
+            if c1 <= c0:
+                continue
+            p0, p1 = c0 // span, (c1 - 1) // span + 1
+            column = c0 + lax.broadcasted_iota(jnp.int32, (1, c1 - c0), 1)
+            part = jnp.concatenate(
+                [p[group * piece : group * (piece + 1), : c1 - c0] for p in parts], 0
+            )
+            masked, left = [], []
+            for pair in range(p0, p1):
+                split = pair * span + TRUNC + 1 - waves_ref[me * slots + 2 * pair]
+                low = (column >= pair * span) & (column < split)
+                high = (column >= split) & (column < (pair + 1) * span)
+                masked.append(jnp.where(low, part, 0.0))
+                masked.append(jnp.where(high, part, 0.0))
+                left.append(held_ref[pl.ds(2 * pair, rows, stride=slots), :])
+                left.append(held_ref[pl.ds(2 * pair + 1, rows, stride=slots), :])
+            right = jnp.concatenate(masked, 0).astype(BF16)
+            out_ref[:, c0:c1] = dot(jnp.concatenate(left, 0).astype(BF16), right, 0, 0)
 
 
 def sine_turns(v):
@@ -118,13 +154,13 @@
     each = MS // RADIX
     column = lax.broadcasted_iota(jnp.int32, (MS, MS), 1)
     wave = M0 + RADIX * (column % each) + column // each
-    return (waves == wave).astype(F32).astype(BF16)
+    return (waves == wave.astype(F32)).astype(F32).astype(BF16)
 
 
 def transform_kernel(
-    owners, groups, points_ref, weight_ref, waves_ref, four_ref, factor_ref,
-    out_ref, came_ref, leave_ref, acc_ref, high_ref, low_ref, turn_ref,
-    send_four, recv_four, send_back, recv_back,
+    owners, groups, points_ref, weight_ref, waves_ref, four_ref, factor_ref, leg_ref,
+    out_ref, table_ref, came_ref, leave_ref, acc_ref, high_ref, low_ref, turn_ref,
+    send_four, recv_four, send_back, recv_back, send_leg, recv_leg,
 ):
     me, here = lax.axis_index("wave"), lax.axis_index("lat")
     lats = lax.axis_size("lat")
@@ -153,12 +189,30 @@
         four_copy(step, lax.rem(me + step, owners), me).start()
     came_ref[me] = four_ref[me]
 
+    sibling = here + 1 - 2 * lax.rem(here, 2)
+
+    def leg_copy(at, source, row, to):
+        return pltpu.make_async_remote_copy(
+            src_ref=source,
+            dst_ref=table_ref.at[row],
+            send_sem=send_leg.at[at],
+            recv_sem=recv_leg.at[row],
+            device_id=(me, to),
+            device_id_type=MESH,
+        )
+
+    if groups > 1:
+        for step in range(2, groups, 2):
+            leg_copy(step, leg_ref, here, lax.rem(here + step, lats)).start()
+        leg_copy(0, leg_ref, here, sibling).start()
+    table_ref[here if groups > 1 else 0] = leg_ref[...]
+
     count = points_ref[0, me].astype(F32)
     scale = weight_ref[0, me] / count
     quarter = count * 0.25
     levels = four_ref.shape[1] // 2
     each = MS // RADIX
-    order = order_matrix(waves_ref[...])
+    order = order_matrix(wave_column(waves_ref))
 
     def make_tables(index, carry):
         start = index * CHUNK
@@ -257,6 +311,18 @@
     for step, offset in enumerate(offsets):
         back_copy(step, peer(offset), base + me).start()
     out_ref[base + me] = leave_ref[me]
+    if groups > 1:
+        for step in range(2, groups, 2):
+            row = lax.rem(here + lats - step, lats)
+            leg_copy(step, leg_ref, row, row).wait_recv()
+            leg_copy(step + 1, table_ref.at[row], row, sibling).start()
+        for step in range(0, groups, 2):
+            leg_copy(step, leg_ref, here, sibling).wait_send()
+            row = lax.rem(sibling + lats - step, lats)
+            leg_copy(step, leg_ref, row, sibling).wait_recv()
+        for step in range(2, groups, 2):
+            row = lax.rem(here + lats - step, lats)
+            leg_copy(step + 1, table_ref.at[row], row, sibling).wait_send()
     for step, offset in enumerate(offsets):
         back_copy(step, peer(offset), base + me).wait_send()
         source = lax.rem(me + owners - offset[0], owners), lax.rem(here + lats - offset[1], lats)
@@ -266,6 +332,7 @@
 
 PARAMS = pltpu.CompilerParams(vmem_limit_bytes=40 * 1024 * 1024)
 VMEM = pl.BlockSpec(memory_space=pltpu.VMEM)
+HBM = pl.BlockSpec(memory_space=pltpu.HBM)
 SMEM = pl.BlockSpec(memory_space=pltpu.SMEM)
 
 
@@ -277,32 +344,46 @@
     per_owner = MS // owners
     group, own = legendre.shape
     span = own // (per_owner // 2)
-    gather = groups * group * legendre.dtype.itemsize < 2 * chans * 4
-    table = lax.all_gather(legendre, "lat") if gather else legendre[None]
-    waves = wave_of_slot[:, None]
+    gather = groups % 2 == 0 and groups * group * legendre.dtype.itemsize < 2 * chans * 4
+    pieces = max(1, 16 // group)
+    packed = -(-own // (pieces * 128)) * 128
+    waves = wave_of_slot[None]
     coeffs = spectral.reshape(chans, own)
     length = grid_factor.shape[2]
     padded = -(-(length // RADIX) // CHUNK) * CHUNK
     wide = -(-length // 128) * 128
-    fourier, factors = pl.pallas_call(
+    fourier, factors, mine = pl.pallas_call(
         functools.partial(prepare_kernel, span),
         out_shape=[
             jax.ShapeDtypeStruct((group, chans, per_owner), BF16),
             jax.ShapeDtypeStruct((RADIX, padded), F32),
+            jax.ShapeDtypeStruct((pieces * group, packed), BF16),
         ],
-        in_specs=[SMEM] + [VMEM] * 4,
-        out_specs=[VMEM] * 2,
-        scratch_shapes=[pltpu.VMEM((group, per_owner, chans), F32), pltpu.VMEM((1, wide), F32)],
-        compiler_params=PARAMS,
+        in_specs=[SMEM, VMEM] + [HBM] * 3,
+        out_specs=[VMEM] * 3,
+        scratch_shapes=[
+            pltpu.VMEM((group, per_owner, chans), F32),
+            pltpu.VMEM((1, wide), F32),
+            pltpu.VMEM((MS, 1), jnp.int32),
+            pltpu.VMEM((pieces * group, packed), F32),
+            pltpu.VMEM((chans, own), BF16),
+            pltpu.VMEM((group, own), BF16),
+            pltpu.VMEM(grid_factor.shape[1:], F32),
+            pltpu.SemaphoreType.DMA((3,)),
+        ],
+        compiler_params=pltpu.CompilerParams(vmem_limit_bytes=62 * 1024 * 1024),
         name="prepare",
     )(row_points, waves, coeffs, legendre, grid_factor[0])
     used = groups if gather else 1
     others = owners * used - 1
-    back = pl.pallas_call(
+    back, table = pl.pallas_call(
         functools.partial(transform_kernel, owners, used),
-        out_shape=jax.ShapeDtypeStruct((owners * used, chans, per_owner), BF16),
-        in_specs=[SMEM] * 2 + [VMEM] * 3,
-        out_specs=VMEM,
+        out_shape=[
+            jax.ShapeDtypeStruct((owners * used, chans, per_owner), BF16),
+            jax.ShapeDtypeStruct((used, pieces * group, packed), BF16),
+        ],
+        in_specs=[SMEM] * 2 + [VMEM] * 4,
+        out_specs=[VMEM] * 2,
         scratch_shapes=[
             pltpu.VMEM((owners, chans, per_owner), BF16),
             pltpu.VMEM((owners, chans, per_owner), BF16),
@@ -314,14 +395,16 @@
             pltpu.SemaphoreType.DMA((owners,)),
             pltpu.SemaphoreType.DMA((others,)),
             pltpu.SemaphoreType.DMA((owners * used,)),
+            pltpu.SemaphoreType.DMA((max(used, 2),)),
+            pltpu.SemaphoreType.DMA((used,)),
         ],
         compiler_params=pltpu.CompilerParams(
             collective_id=0, has_side_effects=True, vmem_limit_bytes=40 * 1024 * 1024
         ),
         name="transform",
-    )(row_points, quad_weight, waves, fourier, factors)
+    )(row_points, quad_weight, waves, fourier, factors, mine)
     out = pl.pallas_call(
-        functools.partial(output_kernel, span),
+        functools.partial(output_kernel, span, group),
         out_shape=jax.ShapeDtypeStruct((chans, own), F32),
         in_specs=[SMEM] + [VMEM] * 2,
         out_specs=VMEM,

time: 55.2 us -> 39 us (0.71)
  between operations: 13.4 us -> 0.05 us
  Pallas kernels: 30.7 us -> 36.1 us
  waiting for transfers between devices: 4.21 us -> 0 us
  local copies, waits for them, and re-layouts: 6.56 us -> 2.55 us
    all_gather x1 -> x0, waiting for transfers between devices: 3.5 us -> none  [on_device(): table = lax.all_gather(legendre, 'lat') if gather else legendre[None]]
    unnamed x14 -> x12, local copies, waits for them, and re-layouts: 5.74 us -> 2.55 us
    pallas_call x1, Pallas kernels: 2 us -> 4.66 us  [on_device(): pl.pallas_call(functools.partial(prepare_kernel, span), out_shape=[jax.Sh...]
    pallas_call x1, Pallas kernels: 23.5 us -> 25.1 us  [on_device(): pl.pallas_call(functools.partial(transform_kernel, owners, used), out_sha...]
    pallas_call x1, Pallas kernels: 5.22 us -> 6.34 us  [on_device(): pl.pallas_call(functools.partial(output_kernel, span, group), out_shape=j...]
    broadcast_in_dim x1 -> x0, local copies, waits for them, and re-layouts: 0.82 us -> none  [on_device(): waves = wave_of_slot[:, None]]
    unnamed x1 -> x0, waiting for transfers between devices: 0.71 us -> none
  transfers between devices with their start and end apart: 1 -> 0, of which waited for: 1 -> 0; matrix products, arithmetic and copies ran while one was open for 1% -> 0% of each run, Pallas kernels for 46% -> 0%
where the time goes in v3:
time: 39 us; the launch traced here: 38.7 us
  Pallas kernels  36.1 us (93%)
  local copies, waits for them, and re-layouts  2.55 us (7%)
    pallas_call x1, Pallas kernels, on_device(): pl.pallas_call(functools.partial(transform_kernel, owners, used), out_sha...  25.1 us
    pallas_call x1, Pallas kernels, on_device(): pl.pallas_call(functools.partial(output_kernel, span, group), out_shape=j...  6.34 us
    pallas_call x1, Pallas kernels, on_device(): pl.pallas_call(functools.partial(prepare_kernel, span), out_shape=[jax.Sh...  4.66 us
    unnamed x12, local copies, waits for them, and re-layouts  2.55 us

profile of v3, /device:TPU:0, one launch (start us, length us, event | category | flops | bytes accessed | tf_op | source)
XLA Modules:
  0.0 38.7 jit_solution(7033513415601166931)
XLA Ops:
  0.0 0.0 copy-start.4
  0.0 0.0 copy-start.3
  0.0 0.0 copy-start.5
  0.0 4.7 %prepare.1 = (bf16[4,32,128]{2,1,0:T(8,128)(2,1)}, f32[4,4096]{1,0:T(4,128)}, bf16[16,8320]{1,0:T(8,128)(2,1)}) custom-call(s32[1,4]{1,0:T(1,128)} %points_ref.3, s32[1,512]{1,0:T(1,128)} %bitcast.4, bf16[32,32832]{1,0:T(8,128)(2,1)} %bitcast.6, bf16[4,32832]{1,0:T(4,128)(2,1)} %leg_hbm.1, f32[4,16016]{1,0:T(4,128)} %bitcast.7), custom_call_target="tpu_custom_call" | custom-call | tf_op jit(solution)/shard_map/prepare/pallas_call | solution.py:355
  4.7 0.0 copy-done.4
  4.7 0.0 copy-done.3
  4.7 0.0 copy-done.5
  4.7 0.0 copy-start
  4.7 0.9 %copy-done = bf16[16,8320]{1,0:T(8,128)(2,1)S(1)} copy-done((bf16[16,8320]{1,0:T(8,128)(2,1)S(1)}, bf16[16,8320]{1,0:T(8,128)(2,1)}, u32[]{:S(2)}) %copy-start) | copy-done | bytes 266264
  5.7 0.0 copy-start.1
  5.7 0.8 %copy-done.1 = f32[4,4096]{1,0:T(4,128)S(1)} copy-done((f32[4,4096]{1,0:T(4,128)S(1)}, f32[4,4096]{1,0:T(4,128)}, u32[]{:S(2)}) %copy-start.1) | copy-done | bytes 65560
  6.5 0.0 copy-start.2
  6.5 0.8 %copy-done.2 = bf16[4,32,128]{2,1,0:T(8,128)(2,1)S(1)} copy-done((bf16[4,32,128]{2,1,0:T(8,128)(2,1)S(1)}, bf16[4,32,128]{2,1,0:T(8,128)(2,1)}, u32[]{:S(2)}) %copy-start.2) | copy-done | bytes 32792
  7.3 25.1 %transform.1 = (bf16[32,32,128]{2,1,0:T(8,128)(2,1)S(1)}, bf16[8,16,8320]{2,1,0:T(8,128)(2,1)S(1)}) custom-call(s32[1,4]{1,0:T(1,128)S(1)} %copy-done.4, f32[1,4]{1,0:T(1,128)S(1)} %copy-done.5, s32[1,512]{1,0:T(1,128)S(1)} %bitcast.5, bf16[4,32,128]{2,1,0:T(8,128)(2,1)S(1)} %copy-done.2, f32[4,4096]{1,0:T(4,128)S(1)} %copy-done.1, bf16[16,8320]{1,0:T(8,128)(2,1)S(1)} %copy-done), custom_call_target="tpu_custom_call" | custom-call | tf_op jit(solution)/shard_map/transform/pallas_call | solution.py:379
  32.4 6.3 %output.1 = f32[32,32832]{1,0:T(8,128)} custom-call(s32[512]{0:T(512)S(1)} %copy-done.3, bf16[8,16,8320]{2,1,0:T(8,128)(2,1)S(1)} %get-tuple-element.13.leg_ref, bf16[32,32,128]{2,1,0:T(8,128)(2,1)S(1)} %get-tuple-element.14.back_ref), custom_call_target="tpu_custom_call" | custom-call | tf_op jit(solution)/shard_map/output/pallas_call | solution.py:406
Async XLA Ops:
  0.0 4.7 %copy-start.4 = (s32[1,4]{1,0:T(1,128)S(1)}, s32[1,4]{1,0:T(1,128)}, u32[]{:S(2)}) copy-start(s32[1,4]{1,0:T(1,128)} %points_ref.3) | copy-start | bytes 52
  0.0 4.7 %copy-start.3 = (s32[512]{0:T(512)S(1)}, s32[512]{0:T(512)}, u32[]{:S(2)}) copy-start(s32[512]{0:T(512)} %waves_ref.1) | copy-start | bytes 6148
  0.0 4.7 %copy-start.5 = (f32[1,4]{1,0:T(1,128)S(1)}, f32[1,4]{1,0:T(1,128)}, u32[]{:S(2)}) copy-start(f32[1,4]{1,0:T(1,128)} %weight_ref.1) | copy-start | bytes 52
  4.7 1.0 %copy-start = (bf16[16,8320]{1,0:T(8,128)(2,1)S(1)}, bf16[16,8320]{1,0:T(8,128)(2,1)}, u32[]{:S(2)}) copy-start(bf16[16,8320]{1,0:T(8,128)(2,1)} %get-tuple-element.12.leg_ref) | copy-start | bytes 798724
  5.7 0.8 %copy-start.1 = (f32[4,4096]{1,0:T(4,128)S(1)}, f32[4,4096]{1,0:T(4,128)}, u32[]{:S(2)}) copy-start(f32[4,4096]{1,0:T(4,128)} %get-tuple-element.11.factor_ref) | copy-start | bytes 196612
  6.5 0.8 %copy-start.2 = (bf16[4,32,128]{2,1,0:T(8,128)(2,1)S(1)}, bf16[4,32,128]{2,1,0:T(8,128)(2,1)}, u32[]{:S(2)}) copy-start(bf16[4,32,128]{2,1,0:T(8,128)(2,1)} %get-tuple-element.10.four_ref) | copy-start | bytes 98308

commit v4 on v3

--- a/solution.py
+++ b/solution.py
@@ -38,22 +38,7 @@
     return jnp.broadcast_to(row, (8, row.shape[1])).T[:, :1]
 
 
-def prepare_kernel(
-    span, points_ref, waves_ref, spec_hbm, leg_hbm, grid_hbm, out_ref, factor_ref, packed_ref,
-    acc_ref, row_ref, column_ref, pack_ref, spec_ref, leg_ref, grid_ref, sems,
-):
-    me = lax.axis_index("wave")
-    copies = [
-        pltpu.make_async_copy(source, target, sems.at[i])
-        for i, (source, target) in enumerate(
-            ((spec_hbm, spec_ref), (leg_hbm, leg_ref), (grid_hbm, grid_ref))
-        )
-    ]
-    for copy in copies:
-        copy.start()
-    column_ref[...] = wave_column(waves_ref).astype(jnp.int32)
-    for copy in copies:
-        copy.wait()
+def pack_rows(leg_ref, pack_ref, packed_ref):
     group, own = leg_ref.shape
     length = packed_ref.shape[1]
     for piece in range(packed_ref.shape[0] // group):
@@ -64,6 +49,10 @@
             :, first:last
         ].astype(F32)
     packed_ref[...] = pack_ref[...].astype(BF16)
+
+
+def make_fourier(span, me, column_ref, spec_ref, leg_ref, acc_ref, out_ref):
+    group, own = leg_ref.shape
     slots = acc_ref.shape[1]
     for first in range(0, slots, 8):
         c0 = first // 2 * span // 128 * 128
@@ -81,11 +70,11 @@
             acc_ref[r, first : first + 8, :] = sums[8 * r : 8 * r + 8, :]
     for r in range(group):
         out_ref[r] = acc_ref[r].T.astype(BF16)
+
+
+def shift_factors(quarter, row_ref, factor_ref):
     wide = row_ref.shape[1]
-    row_ref[...] = jnp.zeros_like(row_ref)
-    row_ref[:, : grid_ref.shape[1]] = grid_ref[pl.ds(me, 1), :]
     row = row_ref[...]
-    quarter = points_ref[0, me] // RADIX
     for t in range(RADIX):
         shifted = pltpu.roll(row, wide - t * quarter, 1) if t else row
         factor_ref[t : t + 1, :] = shifted[:, : factor_ref.shape[1]]
@@ -158,8 +147,9 @@
 
 
 def transform_kernel(
-    owners, groups, points_ref, weight_ref, waves_ref, four_ref, factor_ref, leg_ref,
-    out_ref, table_ref, came_ref, leave_ref, acc_ref, high_ref, low_ref, turn_ref,
+    span, owners, groups, points_ref, weight_ref, waves_ref, spec_hbm, rows_hbm, grid_hbm,
+    out_ref, table_ref, four_ref, factor_ref, leg_ref,
+    sums_ref, row_ref, column_ref, pack_ref, spec_ref, rows_ref, grid_ref, sems, came_ref, leave_ref, acc_ref, high_ref, low_ref, turn_ref,
     send_four, recv_four, send_back, recv_back, send_leg, recv_leg,
 ):
     me, here = lax.axis_index("wave"), lax.axis_index("lat")
@@ -170,9 +160,20 @@
     def peer(offset):
         return lax.rem(me + offset[0], owners), lax.rem(here + offset[1], lats)
 
+    loads = [
+        pltpu.make_async_copy(source, target, sems.at[i])
+        for i, (source, target) in enumerate(
+            ((rows_hbm, rows_ref), (spec_hbm, spec_ref), (grid_hbm, grid_ref))
+        )
+    ]
+    for load in loads:
+        load.start()
     barrier = pltpu.get_barrier_semaphore()
     for offset in offsets:
         pl.semaphore_signal(barrier, inc=1, device_id=peer(offset), device_id_type=MESH)
+    column_ref[...] = wave_column(waves_ref).astype(jnp.int32)
+    loads[0].wait()
+    pack_rows(rows_ref, pack_ref, leg_ref)
     pl.semaphore_wait(barrier, len(offsets))
 
     def four_copy(step, to, owner):
@@ -185,10 +186,6 @@
             device_id_type=MESH,
         )
 
-    for step in range(1, owners):
-        four_copy(step, lax.rem(me + step, owners), me).start()
-    came_ref[me] = four_ref[me]
-
     sibling = here + 1 - 2 * lax.rem(here, 2)
 
     def leg_copy(at, source, row, to):
@@ -205,7 +202,16 @@
         for step in range(2, groups, 2):
             leg_copy(step, leg_ref, here, lax.rem(here + step, lats)).start()
         leg_copy(0, leg_ref, here, sibling).start()
+    loads[1].wait()
+    make_fourier(span, me, column_ref, spec_ref, rows_ref, sums_ref, four_ref)
+    for step in range(1, owners):
+        four_copy(step, lax.rem(me + step, owners), me).start()
+    came_ref[me] = four_ref[me]
     table_ref[here if groups > 1 else 0] = leg_ref[...]
+    loads[2].wait()
+    row_ref[...] = jnp.zeros_like(row_ref)
+    row_ref[:, : grid_ref.shape[1]] = grid_ref[pl.ds(me, 1), :]
+    shift_factors(points_ref[0, me] // RADIX, row_ref, factor_ref)
 
     count = points_ref[0, me].astype(F32)
     scale = weight_ref[0, me] / count
@@ -352,16 +358,20 @@
     length = grid_factor.shape[2]
     padded = -(-(length // RADIX) // CHUNK) * CHUNK
     wide = -(-length // 128) * 128
-    fourier, factors, mine = pl.pallas_call(
-        functools.partial(prepare_kernel, span),
+    used = groups if gather else 1
+    others = owners * used - 1
+    back, table = pl.pallas_call(
+        functools.partial(transform_kernel, span, owners, used),
         out_shape=[
-            jax.ShapeDtypeStruct((group, chans, per_owner), BF16),
-            jax.ShapeDtypeStruct((RADIX, padded), F32),
-            jax.ShapeDtypeStruct((pieces * group, packed), BF16),
+            jax.ShapeDtypeStruct((owners * used, chans, per_owner), BF16),
+            jax.ShapeDtypeStruct((used, pieces * group, packed), BF16),
         ],
-        in_specs=[SMEM, VMEM] + [HBM] * 3,
-        out_specs=[VMEM] * 3,
+        in_specs=[SMEM] * 2 + [VMEM] + [HBM] * 3,
+        out_specs=[VMEM] * 2,
         scratch_shapes=[
+            pltpu.VMEM((group, chans, per_owner), BF16),
+            pltpu.VMEM((RADIX, padded), F32),
+            pltpu.VMEM((pieces * group, packed), BF16),
             pltpu.VMEM((group, per_owner, chans), F32),
             pltpu.VMEM((1, wide), F32),
             pltpu.VMEM((MS, 1), jnp.int32),
@@ -370,21 +380,6 @@
             pltpu.VMEM((group, own), BF16),
             pltpu.VMEM(grid_factor.shape[1:], F32),
             pltpu.SemaphoreType.DMA((3,)),
-        ],
-        compiler_params=pltpu.CompilerParams(vmem_limit_bytes=62 * 1024 * 1024),
-        name="prepare",
-    )(row_points, waves, coeffs, legendre, grid_factor[0])
-    used = groups if gather else 1
-    others = owners * used - 1
-    back, table = pl.pallas_call(
-        functools.partial(transform_kernel, owners, used),
-        out_shape=[
-            jax.ShapeDtypeStruct((owners * used, chans, per_owner), BF16),
-            jax.ShapeDtypeStruct((used, pieces * group, packed), BF16),
-        ],
-        in_specs=[SMEM] * 2 + [VMEM] * 4,
-        out_specs=[VMEM] * 2,
-        scratch_shapes=[
             pltpu.VMEM((owners, chans, per_owner), BF16),
             pltpu.VMEM((owners, chans, per_owner), BF16),
             pltpu.VMEM((7 * levels, 2 * MS // RADIX), F32),
@@ -399,10 +394,10 @@
             pltpu.SemaphoreType.DMA((used,)),
         ],
         compiler_params=pltpu.CompilerParams(
-            collective_id=0, has_side_effects=True, vmem_limit_bytes=40 * 1024 * 1024
+            collective_id=0, has_side_effects=True, vmem_limit_bytes=60 * 1024 * 1024
         ),
         name="transform",
-    )(row_points, quad_weight, waves, fourier, factors, mine)
+    )(row_points, quad_weight, waves, coeffs, legendre, grid_factor[0])
     out = pl.pallas_call(
         functools.partial(output_kernel, span, group),
         out_shape=jax.ShapeDtypeStruct((chans, own), F32),

time: 39 us -> 35.7 us (0.915)
  Pallas kernels: 36.1 us -> 32.9 us
    pallas_call x2 -> x1, Pallas kernels: 29.8 us -> 26.5 us  [on_device(): pl.pallas_call(functools.partial(transform_kernel, span, owners, used), o...]
    unnamed x12 -> x6, local copies, waits for them, and re-layouts: 2.55 us -> 2.55 us
where the time goes in v4:
time: 35.7 us; the launch traced here: 35.5 us
  Pallas kernels  32.9 us (92%)
  local copies, waits for them, and re-layouts  2.55 us (7%)
    pallas_call x1, Pallas kernels, on_device(): pl.pallas_call(functools.partial(transform_kernel, span, owners, used), o...  26.5 us
    pallas_call x1, Pallas kernels, on_device(): pl.pallas_call(functools.partial(output_kernel, span, group), out_shape=j...  6.38 us
    unnamed x6, local copies, waits for them, and re-layouts  2.55 us

profile of v4, /device:TPU:0, one launch (start us, length us, event | category | flops | bytes accessed | tf_op | source)
XLA Modules:
  0.0 35.5 jit_solution(31010849830177682)
XLA Ops:
  0.0 0.0 copy-start.2
  0.0 26.5 %transform.1 = (bf16[32,32,128]{2,1,0:T(8,128)(2,1)}, bf16[8,16,8320]{2,1,0:T(8,128)(2,1)}) custom-call(s32[1,4]{1,0:T(1,128)} %points_ref.1, f32[1,4]{1,0:T(1,128)} %weight_ref.1, s32[1,512]{1,0:T(1,128)} %bitcast.4, bf16[32,32832]{1,0:T(8,128)(2,1)} %bitcast.5, bf16[4,32832]{1,0:T(4,128)(2,1)} %rows_hbm.1, f32[4,16016]{1,0:T(4,128)} %bitcast.6), custom_call_target="tpu_custom_call" | custom-call | tf_op jit(solution)/shard_map/transform/pallas_call | solution.py:363
  26.5 0.0 copy-done.2
  26.6 0.0 copy-start
  26.6 1.6 %copy-done = bf16[8,16,8320]{2,1,0:T(8,128)(2,1)S(1)} copy-done((bf16[8,16,8320]{2,1,0:T(8,128)(2,1)S(1)}, bf16[8,16,8320]{2,1,0:T(8,128)(2,1)}, u32[]{:S(2)}) %copy-start) | copy-done | bytes 2129944
  28.2 0.0 copy-start.1
  28.2 0.9 %copy-done.1 = bf16[32,32,128]{2,1,0:T(8,128)(2,1)S(1)} copy-done((bf16[32,32,128]{2,1,0:T(8,128)(2,1)S(1)}, bf16[32,32,128]{2,1,0:T(8,128)(2,1)}, u32[]{:S(2)}) %copy-start.1) | copy-done | bytes 262168
  29.1 6.4 %output.1 = f32[32,32832]{1,0:T(8,128)} custom-call(s32[512]{0:T(512)S(1)} %copy-done.2, bf16[8,16,8320]{2,1,0:T(8,128)(2,1)S(1)} %copy-done, bf16[32,32,128]{2,1,0:T(8,128)(2,1)S(1)} %copy-done.1), custom_call_target="tpu_custom_call" | custom-call | tf_op jit(solution)/shard_map/output/pallas_call | solution.py:401
Async XLA Ops:
  0.0 26.5 %copy-start.2 = (s32[512]{0:T(512)S(1)}, s32[512]{0:T(512)}, u32[]{:S(2)}) copy-start(s32[512]{0:T(512)} %waves_ref.1) | copy-start | bytes 6148
  26.6 1.6 %copy-start = (bf16[8,16,8320]{2,1,0:T(8,128)(2,1)S(1)}, bf16[8,16,8320]{2,1,0:T(8,128)(2,1)}, u32[]{:S(2)}) copy-start(bf16[8,16,8320]{2,1,0:T(8,128)(2,1)} %get-tuple-element.7.leg_ref) | copy-start | bytes 6389764
  28.2 0.9 %copy-start.1 = (bf16[32,32,128]{2,1,0:T(8,128)(2,1)S(1)}, bf16[32,32,128]{2,1,0:T(8,128)(2,1)}, u32[]{:S(2)}) copy-start(bf16[32,32,128]{2,1,0:T(8,128)(2,1)} %get-tuple-element.8.back_ref) | copy-start | bytes 786436

commit v5 on v4

--- a/solution.py
+++ b/solution.py
@@ -80,14 +80,36 @@
         factor_ref[t : t + 1, :] = shifted[:, : factor_ref.shape[1]]
 
 
-def output_kernel(span, group, waves_ref, leg_ref, back_ref, out_ref, held_ref):
+def output_kernel(
+    span, group, waves_ref, leg_hbm, back_hbm, out_hbm, held_ref, leg_ref, back_ref, out_ref, sems
+):
     me = lax.axis_index("wave")
+    load_back = pltpu.make_async_copy(back_hbm, back_ref, sems.at[0])
+    load_leg = pltpu.make_async_copy(leg_hbm, leg_ref, sems.at[1])
+    load_back.start()
+    load_leg.start()
+    load_back.wait()
     groups, packed, length = leg_ref.shape
     own = out_ref.shape[1]
     rows, _, slots = back_ref.shape
     for r in range(rows):
         held_ref[slots * r : slots * (r + 1), :] = back_ref[r].astype(F32).T
+    load_leg.wait()
+    half = length // CHUNK // 2 * CHUNK
+    stores = []
+
+    def store(begin, end):
+        for piece in range(packed // group):
+            c0, c1 = piece * length + begin, min(piece * length + end, own)
+            copy = pltpu.make_async_copy(
+                out_ref.at[:, c0:c1], out_hbm.at[:, c0:c1], sems.at[2 + len(stores)]
+            )
+            copy.start()
+            stores.append(copy)
+
     for at in range(0, length, CHUNK):
+        if at == half:
+            store(0, half)
         parts = [leg_ref[g, :, at : min(at + CHUNK, length)].astype(F32) for g in range(groups)]
         for piece in range(packed // group):
             c0 = piece * length + at
@@ -110,6 +132,9 @@
                 left.append(held_ref[pl.ds(2 * pair + 1, rows, stride=slots), :])
             right = jnp.concatenate(masked, 0).astype(BF16)
             out_ref[:, c0:c1] = dot(jnp.concatenate(left, 0).astype(BF16), right, 0, 0)
+    store(half, length)
+    for copy in stores:
+        copy.wait()
 
 
 def sine_turns(v):
@@ -336,7 +361,6 @@
         back_copy(step, source, row).wait_recv()
 
 
-PARAMS = pltpu.CompilerParams(vmem_limit_bytes=40 * 1024 * 1024)
 VMEM = pl.BlockSpec(memory_space=pltpu.VMEM)
 HBM = pl.BlockSpec(memory_space=pltpu.HBM)
 SMEM = pl.BlockSpec(memory_space=pltpu.SMEM)
@@ -401,10 +425,16 @@
     out = pl.pallas_call(
         functools.partial(output_kernel, span, group),
         out_shape=jax.ShapeDtypeStruct((chans, own), F32),
-        in_specs=[SMEM] + [VMEM] * 2,
-        out_specs=VMEM,
-        scratch_shapes=[pltpu.VMEM((owners * used * per_owner, chans), F32)],
-        compiler_params=PARAMS,
+        in_specs=[SMEM] + [HBM] * 2,
+        out_specs=HBM,
+        scratch_shapes=[
+            pltpu.VMEM((owners * used * per_owner, chans), F32),
+            pltpu.VMEM((used, pieces * group, packed), BF16),
+            pltpu.VMEM((owners * used, chans, per_owner), BF16),
+            pltpu.VMEM((chans, own), F32),
+            pltpu.SemaphoreType.DMA((2 + 2 * pieces,)),
+        ],
+        compiler_params=pltpu.CompilerParams(vmem_limit_bytes=62 * 1024 * 1024),
         name="output",
     )(wave_of_slot, table, back)
     if not gather:

time: 35.7 us -> 33.9 us (0.950)
  local copies, waits for them, and re-layouts: 2.55 us -> 0 us
  Pallas kernels: 32.9 us -> 33.6 us
    unnamed x6 -> x0, local copies, waits for them, and re-layouts: 2.55 us -> none
    pallas_call x1, Pallas kernels: 6.38 us -> 7.22 us  [on_device(): pl.pallas_call(functools.partial(output_kernel, span, group), out_shape=j...]
where the time goes in v5:
time: 33.9 us; the launch traced here: 33.7 us
  Pallas kernels  33.6 us (99%)
    pallas_call x1, Pallas kernels, on_device(): pl.pallas_call(functools.partial(transform_kernel, span, owners, used), o...  26.4 us
    pallas_call x1, Pallas kernels, on_device(): pl.pallas_call(functools.partial(output_kernel, span, group), out_shape=j...  7.22 us

profile of v5, /device:TPU:0, one launch (start us, length us, event | category | flops | bytes accessed | tf_op | source)
XLA Modules:
  0.0 33.7 jit_solution(14873962907231500346)
XLA Ops:
  0.0 26.4 %transform.1 = (bf16[32,32,128]{2,1,0:T(8,128)(2,1)}, bf16[8,16,8320]{2,1,0:T(8,128)(2,1)}) custom-call(s32[1,4]{1,0:T(1,128)} %points_ref.1, f32[1,4]{1,0:T(1,128)} %weight_ref.1, s32[1,512]{1,0:T(1,128)} %bitcast.6, bf16[32,32832]{1,0:T(8,128)(2,1)} %bitcast.4, bf16[4,32832]{1,0:T(4,128)(2,1)} %rows_hbm.1, f32[4,16016]{1,0:T(4,128)} %bitcast.5), custom_call_target="tpu_custom_call" | custom-call | tf_op jit(solution)/shard_map/transform/pallas_call | solution.py:387
  26.4 7.2 %output.1 = f32[32,32832]{1,0:T(8,128)} custom-call(s32[512]{0:T(512)} %waves_ref.1, bf16[8,16,8320]{2,1,0:T(8,128)(2,1)} %get-tuple-element.7.leg_hbm, bf16[32,32,128]{2,1,0:T(8,128)(2,1)} %get-tuple-element.8.back_hbm), custom_call_target="tpu_custom_call" | custom-call | tf_op jit(solution)/shard_map/output/pallas_call | solution.py:425

commit v6 on v5

--- a/solution.py
+++ b/solution.py
@@ -314,6 +314,11 @@
         return carry
 
     lax.fori_loop(0, chunks, step, 0)
+    if groups > 1:
+        for hop in range(2, groups, 2):
+            row = lax.rem(here + lats - hop, lats)
+            leg_copy(hop, leg_ref, row, row).wait_recv()
+            leg_copy(hop + 1, table_ref.at[row], row, sibling).start()
     total = acc_ref[...] * scale
     on_cos = [total[levels * i : levels * (i + 1), :each] for i in range(7)]
     on_sin = [total[levels * i : levels * (i + 1), each:] for i in range(7)]
@@ -343,10 +348,6 @@
         back_copy(step, peer(offset), base + me).start()
     out_ref[base + me] = leave_ref[me]
     if groups > 1:
-        for step in range(2, groups, 2):
-            row = lax.rem(here + lats - step, lats)
-            leg_copy(step, leg_ref, row, row).wait_recv()
-            leg_copy(step + 1, table_ref.at[row], row, sibling).start()
         for step in range(0, groups, 2):
             leg_copy(step, leg_ref, here, sibling).wait_send()
             row = lax.rem(sibling + lats - step, lats)

time: 33.9 us -> 38 us (1.12)
  Pallas kernels: 33.6 us -> 37.8 us
    pallas_call x1, Pallas kernels: 26.4 us -> 30.6 us  [on_device(): pl.pallas_call(functools.partial(transform_kernel, span, owners, used), o...]
where the time goes in v6:
time: 38 us; the launch traced here: 37.8 us
  Pallas kernels  37.8 us (99%)
    pallas_call x1, Pallas kernels, on_device(): pl.pallas_call(functools.partial(transform_kernel, span, owners, used), o...  30.6 us
    pallas_call x1, Pallas kernels, on_device(): pl.pallas_call(functools.partial(output_kernel, span, group), out_shape=j...  7.22 us

profile of v6, /device:TPU:0, one launch (start us, length us, event | category | flops | bytes accessed | tf_op | source)
XLA Modules:
  0.0 37.8 jit_solution(958792956187849738)
XLA Ops:
  0.0 30.6 %transform.1 = (bf16[32,32,128]{2,1,0:T(8,128)(2,1)}, bf16[8,16,8320]{2,1,0:T(8,128)(2,1)}) custom-call(s32[1,4]{1,0:T(1,128)} %points_ref.1, f32[1,4]{1,0:T(1,128)} %weight_ref.1, s32[1,512]{1,0:T(1,128)} %bitcast.6, bf16[32,32832]{1,0:T(8,128)(2,1)} %bitcast.4, bf16[4,32832]{1,0:T(4,128)(2,1)} %rows_hbm.1, f32[4,16016]{1,0:T(4,128)} %bitcast.5), custom_call_target="tpu_custom_call" | custom-call | tf_op jit(solution)/shard_map/transform/pallas_call | solution.py:388
  30.6 7.2 %output.1 = f32[32,32832]{1,0:T(8,128)} custom-call(s32[512]{0:T(512)} %waves_ref.1, bf16[8,16,8320]{2,1,0:T(8,128)(2,1)} %get-tuple-element.7.leg_hbm, bf16[32,32,128]{2,1,0:T(8,128)(2,1)} %get-tuple-element.8.back_hbm), custom_call_target="tpu_custom_call" | custom-call | tf_op jit(solution)/shard_map/output/pallas_call | solution.py:426
